TPU v7x, 32 devices: a whole 2x2x4 slice. The times are simulated.
32 devices in a mesh: section: 2 (over core), dp: 16 (over z, y, x).
Axes of the slice: x: 2, y: 2, z: 4, core: 2. Of those that a mesh axis runs over, the one named last changes fastest.
Arguments:
- tokens: bfloat16 [32, 196, 768], P('dp'), may hold values from -6 to 6
- patch_mask: int32 [32, 196], P('dp'), may hold values from 0 to 1, as said below
- cotangent: bfloat16 [2, 32, 196, 768], P('section', 'dp'), may hold values from -6 to 6
- in_weight: bfloat16 [2, 768, 2304], P('section'), may hold values from -0.21875 to 0.21875
- out_weight: bfloat16 [2, 768, 768], P('section'), may hold values from -1.75 to 1.75
- up_weight: bfloat16 [2, 768, 3072], P('section'), may hold values from -0.21875 to 0.21875
- down_weight: bfloat16 [2, 3072, 768], P('section'), may hold values from -0.109375 to 0.109375
- gains: float32 [2, 4, 768], P('section'), may hold values from 0.1 to 1.9
- biases: float32 [2, 5, 768], P('section'), may hold values from -1.8 to 1.8
- up_bias: float32 [2, 3072], P('section'), may hold values from -1.8 to 1.8
- down_bias: float32 [2, 768], P('section'), may hold values from -1.8 to 1.8
Outputs:
- block_outputs: bfloat16 [2, 32, 196, 768], P('section', 'dp')
- token_grads: float32 [2, 32, 196, 768], P('section', 'dp')
- in_grad: float32 [2, 768, 2304], P('section', None, 'dp')
- out_grad: float32 [2, 768, 768], P('section', None, 'dp')
- up_grad: float32 [2, 768, 3072], P('section', None, 'dp')
- down_grad: float32 [2, 3072, 768], P('section', None, 'dp')
- gain_grad: float32 [2, 4, 768], P('section', None, 'dp')
- bias_grad: float32 [2, 5, 768], P('section', None, 'dp')
- up_bias_grad: float32 [2, 3072], P('section', 'dp')
- down_bias_grad: float32 [2, 768], P('section', 'dp')
Inputs may be any that keep to these rules, and one draw needn't show every extreme that they name: `patch_mask`: each image masks between 59 and 117 of its 196 patches; some image masks exactly 59 and another exactly 117.
All inputs are finite; a program needn't handle non-finite values.
Results may differ from a plain program's by a relative error of at most 0.012.
Values may be sent and summed in bfloat16 or wider, within the bound.
No kernel may reach another device: no remote copies, remote signals or barrier semaphores. Data moves between devices by JAX's collectives and lax.ppermute only.
A program may use at most 256 MiB of HBM per device.

v0:
```python
import jax
import jax.numpy as jnp
from jax import lax
from jax.sharding import PartitionSpec as P

HEADS = 12
HEAD_DIM = 64
IMG_MB = 1
MICRO = 2


epsilon = 1e-06


def shifted(value, axis, by):
    length = lax.axis_size(axis)
    pairs = [(i, i + by) for i in range(length) if 0 <= i + by < length]
    return lax.ppermute(value, axis, pairs)


def layer_norm(states, gain, shift):
    centre = states - jnp.mean(states, axis=-1, keepdims=True)
    spread = jnp.mean(centre * centre, axis=-1, keepdims=True)
    return centre * lax.rsqrt(spread + epsilon) * gain + shift


def gelu_exact(values):
    return jax.nn.gelu(values, approximate=False)


def project(left, right):
    return jnp.einsum("bpd,de->bpe", left, right, preferred_element_type=jnp.float32)


def project_back(left, right):
    return jnp.einsum("bpe,de->bpd", left, right, preferred_element_type=jnp.float32)


def outer_rows(left, right):
    return jnp.einsum("bpd,bpe->de", left, right, preferred_element_type=jnp.float32)


def row_total(values):
    return jnp.sum(values, axis=(0, 1))


def pack_grads(grads, parts):
    pieces = []
    for item in grads:
        if item.ndim == 1:
            pieces.append(item.reshape(parts, -1))
        else:
            leading = item.shape[0]
            pieces.append(item.reshape(leading, parts, -1).transpose(1, 0, 2).reshape(parts, -1))
    return jnp.concatenate(pieces, axis=1)


def unpack_grads(flat, shapes, parts):
    results = []
    offset = 0
    for dims in shapes:
        if len(dims) == 1:
            length = dims[0] // parts
            results.append(flat[:, offset : offset + length])
        else:
            length = dims[0] * dims[1] // parts
            results.append(flat[:, offset : offset + length].reshape(1, dims[0], dims[1] // parts))
        offset = offset + length
    return results


def forward_block(states, query_rows, key_rows, weights):
    in_weight, out_weight, up_weight, down_weight, gains, biases, up_bias, down_bias = weights
    images, patches, width = states.shape
    normed = layer_norm(states, gains[0], biases[0]).astype(jnp.bfloat16)
    joined_bias = jnp.concatenate([biases[1], jnp.zeros_like(biases[1]), biases[2]])
    projected = (project(normed, in_weight) + joined_bias).astype(jnp.bfloat16)
    pieces = projected.reshape(images, patches, 3, HEADS, HEAD_DIM)
    queries = pieces[:, :, 0]
    keys_all = pieces[:, :, 1]
    values_all = pieces[:, :, 2]
    scores = jnp.einsum("bqhd,bkhd->bhqk", queries, keys_all, preferred_element_type=jnp.float32)
    logits = jnp.where(key_rows[:, None, None, :] > 0, scores * HEAD_DIM ** (-0.5), -1e30)
    probs = jax.nn.softmax(logits, axis=-1)
    probs_low = probs.astype(jnp.bfloat16)
    mixed = jnp.einsum("bhqk,bkhd->bqhd", probs_low, values_all, preferred_element_type=jnp.float32)
    mixed = mixed.reshape(images, patches, width).astype(jnp.bfloat16)
    attended = project(mixed, out_weight) + biases[3]
    middle = states + gains[1] * attended * query_rows[..., None]
    hidden_in = layer_norm(middle, gains[2], biases[4]).astype(jnp.bfloat16)
    hidden = project(hidden_in, up_weight) + up_bias
    activated = gelu_exact(hidden).astype(jnp.bfloat16)
    lowered = project(activated, down_weight) + down_bias
    result = middle + gains[3] * lowered * query_rows[..., None]
    kept = (
        normed,
        queries,
        keys_all,
        values_all,
        probs,
        probs_low,
        mixed,
        attended,
        middle,
        hidden_in,
        hidden,
        activated,
        lowered,
    )
    return (result, kept)


def backward_block(states, query_rows, weights, kept, grad_out):
    in_weight, out_weight, up_weight, down_weight, gains, biases, up_bias, down_bias = weights
    (
        normed,
        queries,
        keys_all,
        values_all,
        probs,
        probs_low,
        mixed,
        attended,
        middle,
        hidden_in,
        hidden,
        activated,
        lowered,
    ) = kept
    images, patches, width = states.shape
    rows = query_rows[..., None]
    grad_lowered = (grad_out * gains[3] * rows).astype(jnp.bfloat16)
    grad_scale_two = row_total(grad_out * lowered * rows)
    grad_down_bias = row_total(grad_lowered.astype(jnp.float32))
    grad_down = outer_rows(activated, grad_lowered)
    grad_activated = project_back(grad_lowered, down_weight)
    unused, gelu_back = jax.vjp(gelu_exact, hidden)
    grad_hidden = gelu_back(grad_activated)[0].astype(jnp.bfloat16)
    grad_up_bias = row_total(grad_hidden.astype(jnp.float32))
    grad_up = outer_rows(hidden_in, grad_hidden)
    grad_hidden_in = project_back(grad_hidden, up_weight)
    unused, second_back = jax.vjp(layer_norm, middle, gains[2], biases[4])
    grad_middle, grad_gain_two, grad_bias_two = second_back(grad_hidden_in)
    grad_middle = grad_middle + grad_out
    grad_attended = (grad_middle * gains[1] * rows).astype(jnp.bfloat16)
    grad_scale_one = row_total(grad_middle * attended * rows)
    grad_out_bias = row_total(grad_attended.astype(jnp.float32))
    grad_out_weight = outer_rows(mixed, grad_attended)
    grad_mixed = project_back(grad_attended, out_weight).astype(jnp.bfloat16)
    grad_mixed = grad_mixed.reshape(images, patches, HEADS, HEAD_DIM)
    grad_values = jnp.einsum(
        "bhqk,bqhd->bkhd", probs_low, grad_mixed, preferred_element_type=jnp.float32
    )
    grad_probs = jnp.einsum(
        "bqhd,bkhd->bhqk", grad_mixed, values_all, preferred_element_type=jnp.float32
    )
    centred = grad_probs - jnp.sum(probs * grad_probs, axis=-1, keepdims=True)
    grad_scores = (probs * centred * HEAD_DIM ** (-0.5)).astype(jnp.bfloat16)
    grad_queries = jnp.einsum(
        "bhqk,bkhd->bqhd", grad_scores, keys_all, preferred_element_type=jnp.float32
    )
    grad_keys = jnp.einsum(
        "bhqk,bqhd->bkhd", grad_scores, queries, preferred_element_type=jnp.float32
    )
    grad_joined = jnp.stack([grad_queries, grad_keys, grad_values], axis=2)
    grad_joined = grad_joined.reshape(images, patches, 3 * width).astype(jnp.bfloat16)
    joined_total = row_total(grad_joined.astype(jnp.float32))
    grad_in_weight = outer_rows(normed, grad_joined)
    grad_normed = project_back(grad_joined, in_weight)
    unused, first_back = jax.vjp(layer_norm, states, gains[0], biases[0])
    grad_states, grad_gain_one, grad_bias_one = first_back(grad_normed)
    grad_states = grad_states + grad_middle
    grad_gains = jnp.stack([grad_gain_one, grad_scale_one, grad_gain_two, grad_scale_two])
    grad_biases = jnp.stack(
        [
            grad_bias_one,
            joined_total[:width],
            joined_total[2 * width :],
            grad_out_bias,
            grad_bias_two,
        ]
    )
    return (
        grad_states,
        (
            grad_in_weight,
            grad_out_weight,
            grad_up,
            grad_down,
            grad_gains,
            grad_biases,
            grad_up_bias,
            grad_down_bias,
        ),
    )


def on_device(
    tokens,
    patch_mask,
    cotangent,
    in_weight,
    out_weight,
    up_weight,
    down_weight,
    gains,
    biases,
    up_bias,
    down_bias,
):
    weights = (
        in_weight[0],
        out_weight[0],
        up_weight[0],
        down_weight[0],
        gains[0],
        biases[0],
        up_bias[0],
        down_bias[0],
    )
    shapes = tuple((item.shape for item in weights))
    parts = lax.axis_size("dp")
    is_first = lax.axis_index("section") == 0
    masked_all = patch_mask.astype(jnp.float32)

    def rows_of(index):
        token_block = lax.dynamic_slice_in_dim(tokens, index * IMG_MB, IMG_MB, 0).astype(
            jnp.float32
        )
        masked = lax.dynamic_slice_in_dim(masked_all, index * IMG_MB, IMG_MB, 0)
        query_rows = jnp.where(is_first, 1.0 - masked, masked)
        key_rows = jnp.where(is_first, 1.0 - masked, 1.0)
        return (token_block, masked, query_rows, key_rows)

    saved = jnp.zeros(tokens.shape, jnp.float32)
    results = jnp.zeros(tokens.shape, jnp.bfloat16)
    arrived = jnp.zeros((IMG_MB,) + tokens.shape[1:], jnp.bfloat16)
    for tick in range(MICRO + 1):
        index = jnp.where(is_first, min(tick, MICRO - 1), max(tick - 1, 0))
        token_block, masked, query_rows, key_rows = rows_of(index)
        states = jnp.where(
            is_first | (masked[..., None] > 0), token_block, arrived.astype(jnp.float32)
        )
        output, kept = forward_block(states, query_rows, key_rows, weights)
        saved = lax.dynamic_update_slice_in_dim(saved, states, index * IMG_MB, 0)
        results = lax.dynamic_update_slice_in_dim(
            results, (output * query_rows[..., None]).astype(jnp.bfloat16), index * IMG_MB, 0
        )
        if tick < MICRO:
            arrived = shifted(output.astype(jnp.bfloat16), "section", 1)
    totals = tuple((jnp.zeros(item.shape, jnp.float32) for item in weights))
    flat_sum = None
    token_grads = jnp.zeros(tokens.shape, jnp.float32)
    returned = jnp.zeros((IMG_MB,) + tokens.shape[1:], jnp.bfloat16)
    for tick in range(MICRO + 1):
        index = jnp.where(is_first, min(MICRO - tick, MICRO - 1), max(MICRO - 1 - tick, 0))
        valid = jnp.where(is_first, float(tick >= 1), float(tick < MICRO))
        token_block, masked, query_rows, key_rows = rows_of(index)
        states = lax.dynamic_slice_in_dim(saved, index * IMG_MB, IMG_MB, 0)
        output, kept = forward_block(states, query_rows, key_rows, weights)
        cot_block = lax.dynamic_slice_in_dim(cotangent[0], index * IMG_MB, IMG_MB, 0).astype(
            jnp.float32
        )
        grad_out = cot_block * query_rows[..., None] + jnp.where(
            is_first, returned.astype(jnp.float32), 0.0
        )
        grad_states, grads = backward_block(states, query_rows, weights, kept, grad_out)
        split_grad = jnp.where(
            is_first, grad_states * (1.0 - masked)[..., None], grad_states * masked[..., None]
        )
        token_grads = lax.dynamic_update_slice_in_dim(token_grads, split_grad, index * IMG_MB, 0)
        if tick < MICRO:
            returned = shifted(
                (grad_states * (1.0 - masked)[..., None]).astype(jnp.bfloat16), "section", -1
            )
        scaled = tuple((item * valid for item in grads))
        totals = tuple((left + right for left, right in zip(totals, scaled)))
    flat_sum = lax.psum_scatter(pack_grads(totals, parts), "dp", scatter_dimension=0, tiled=True)
    shards = unpack_grads(flat_sum, shapes, parts)
    return (
        results[None],
        token_grads[None],
        shards[0],
        shards[1],
        shards[2],
        shards[3],
        shards[4],
        shards[5],
        shards[6],
        shards[7],
    )


def solution(mesh):
    return jax.shard_map(
        on_device,
        mesh=mesh,
        in_specs=(
            P("dp", None, None),
            P("dp", None),
            P("section", "dp", None, None),
            P("section", None, None),
            P("section", None, None),
            P("section", None, None),
            P("section", None, None),
            P("section", None, None),
            P("section", None, None),
            P("section", None),
            P("section", None),
        ),
        out_specs=(
            P("section", "dp", None, None),
            P("section", "dp", None, None),
            P("section", None, "dp"),
            P("section", None, "dp"),
            P("section", None, "dp"),
            P("section", None, "dp"),
            P("section", None, "dp"),
            P("section", None, "dp"),
            P("section", "dp"),
            P("section", "dp"),
        ),
        check_vma=False,
    )
```

profile of v0, /device:TPU:0, one launch (start us, length us, event | category | flops | bytes accessed | tf_op | source)
XLA Modules:
  0.0 1425.7 jit_solution(3160885645783970769)
XLA Ops:
  10.9 4.2 fusion.635
  25.0 3.2 convolution_convert_fusion.7
  33.1 11.9 fusion.633
  45.0 3.1 collective-permute-start
  67.4 3.2 convolution_convert_fusion.6
  74.4 11.9 fusion.445
  88.2 4.3 fusion.634
  99.5 4.2 fusion.652
  111.6 3.0 fusion.58
  116.9 4.2 fusion.651
  123.6 3.4 fusion.627
  127.3 8.1 multiply_convert_fusion.5
  149.4 3.1 fusion.333
  152.5 3.0 fusion.428
  155.5 5.6 fusion.336
  161.1 5.6 fusion.339
  166.7 6.8 fusion.609
  173.6 5.0 fusion.454
  182.6 4.7 fusion.405
  191.4 3.3 convert_reduce_fusion.8
  196.8 9.5 multiply_convert_fusion.1
  226.9 5.9 fusion.617
  236.7 5.1 convert_reduce_fusion.1
  251.3 3.1 fusion.334
  254.4 3.0 fusion.431
  257.4 5.7 fusion.342
  263.1 5.7 fusion.345
  268.8 6.6 fusion.606
  279.4 5.5 fusion.614
  284.9 4.1 fusion.401
  290.1 3.0 fusion.59
  295.4 4.1 fusion.653
  310.5 9.8 multiply_convert_fusion
  320.4 5.0 fusion.465
  348.3 3.2 fusion.462
  353.3 5.9 convert_reduce_fusion
  359.3 5.2 fusion.394
  371.5 3.1 fusion.335
  374.6 2.9 fusion.433
  377.5 5.6 fusion.348
  383.2 5.6 fusion.351
  392.7 3.8 fusion.397
  396.6 10.1 multiply_add_fusion.2
  406.6 8.0 copy.180
  414.6 10.5 copy.181
  425.1 21.0 %reshape.2458 = f32[16,110592]{1,0:T(8,128)} reshape(f32[16,768,144]{2,1,0:T(8,128)} %copy.181) | data formatting | bytes 14155776 | tf_op jit(solution)/shard_map/reshape | solution.py:54
  446.1 6.4 constant_dynamic-update-slice_fusion.18
  454.5 5.4 copy.182
  459.9 8.6 reshape.2460
  468.5 12.2 multiply_add_fusion.1
  480.8 9.6 copy.183
  490.3 11.5 copy.184
  501.8 15.1 %reshape.2462 = f32[16,147456]{1,0:T(8,128)} reshape(f32[16,768,192]{2,1,0:T(8,128)} %copy.184) | data formatting | bytes 18874368 | tf_op jit(solution)/shard_map/reshape | solution.py:54
  516.9 12.1 multiply_add_fusion
  529.0 16.5 %copy.185 = f32[3072,16,48]{2,0,1:T(8,128)} copy(f32[3072,16,48]{0,2,1:T(8,128)} %bitcast.784) | data formatting | bytes 18874368 | tf_op jit(solution)/shard_map/reshape | solution.py:54
  545.4 36.6 %reshape.2464 = f32[16,147456]{1,0:T(8,128)} reshape(f32[16,3072,48]{2,1,0:T(8,128)} %bitcast.783) | data formatting | bytes 18874368 | tf_op jit(solution)/shard_map/reshape | solution.py:54
  582.0 4.7 fusion.354
  614.8 3.4 constant_dynamic-update-slice_fusion.17
  618.2 7.4 constant_dynamic-update-slice_fusion.16
  626.8 3.9 constant_dynamic-update-slice_fusion.15
  645.2 730.9 %all-reduce.6.cloned.1.call-done = f32[16,443040]{1,0:T(8,128)} async-done(((f32[16,443040]{1,0:T(8,128)}), f32[16,443040]{1,0:T(8,128)}) %all-reduce.6.cloned.1.call-update) | async-done | bytes 28354576
  1376.0 4.6 dynamic-slice_reduce_fusion.3
  1385.1 3.0 dynamic-slice_reduce_fusion.4
  1391.8 10.3 dynamic-slice_reduce_fusion
  (545 shorter events, 245.0 us)
Async XLA Ops:
  7.2 10.7 copy-start
  7.2 1368.8 %all-reduce.6.cloned.1.call-start = ((), (), s32[]{:S(2)}) async-start(), calls=%async_computation | async-start | bytes 56721408
  10.9 6.4 copy-start.142
  10.9 6.3 copy-start.110
  10.9 6.3 copy-start.111
  45.0 9.7 collective-permute-start
  48.1 6.0 copy-start.87
  48.1 6.6 copy-start.47
  50.4 8.9 copy-start.115
  51.1 8.2 copy-start.143
  86.3 6.2 copy-start.48
  86.3 6.2 copy-start.81
  86.3 8.9 copy-start.116
  86.3 6.2 collective-permute-start.1
  123.6 11.8 slice-start.3
  127.0 16.5 %copy-start.6 = (f32[1,196,768]{2,1,0:T(8,128)}, f32[1,196,768]{2,1,0:T(8,128)S(1)}, u32[]{:S(2)}) copy-start(f32[1,196,768]{2,1,0:T(8,128)S(1)} %get-tuple-element.157) | copy-start | bytes 1806340
  127.0 16.5 %copy-start.85 = (f32[196]{0:T(256)}, f32[196]{0:T(256)S(1)}, u32[]{:S(2)}) copy-start(f32[196]{0:T(256)S(1)} %broadcast_multiply_fusion.4) | copy-start | bytes 2356
  127.2 16.3 %copy-start.104 = (f32[196]{0:T(256)}, f32[196]{0:T(256)S(1)}, u32[]{:S(2)}) copy-start(f32[196]{0:T(256)S(1)} %fusion.517) | copy-start | bytes 2356
  127.3 8.2 slice-start.4
  127.3 8.2 copy-start.44
  127.3 8.2 copy-start.71
  127.3 8.2 copy-start.108
  166.7 6.8 copy-start.18
  166.7 6.8 copy-start.30
  166.7 6.8 copy-start.72
  166.7 6.8 copy-start.79
  189.6 6.3 copy-start.146
  189.6 6.4 copy-start.13
  189.6 7.2 copy-start.154
  194.7 40.1 %collective-permute-start.2 = (bf16[1,196,768]{2,1,0:T(8,128)(2,1)}, bf16[1,196,768]{2,1,0:T(8,128)(2,1)}, u32[]{:S(2)}, u32[]{:S(2)}) collective-permute-start(bf16[1,196,768]{2,1,0:T(8,128)(2,1)} %get-tuple-element.139), channel_id=1, source_target_pairs={{16,0},{17,1},{18,2},{19,3},{20,4},{21,5},{22,6},{23,7},{24,8},{25... | collective-permute-start | bytes 903176 | tf_op jit(solution)/shard_map/ppermute | solution.py:18
  196.0 10.4 copy-start.83
  196.8 9.5 copy-start.102
  196.8 9.5 copy-start.151
  226.9 5.9 copy-start.36
  226.9 5.9 copy-start.58
  226.9 9.7 copy-start.157
  226.9 14.9 %slice-start.9 = ((s8[4718592]{0:T(1024)(128)(4,1)}), s8[4194304]{0:T(1024)(128)(4,1)S(1)}, s32[]{:S(2)}) async-start(s8[4718592]{0:T(1024)(128)(4,1)} %bitcast.865), calls=%async_computation.10 | async-start | bytes 8388608
  234.8 7.0 slice-start.10
  303.7 21.7 %slice-start.5 = ((s8[4718592]{0:T(1024)(128)(4,1)}), s8[4194304]{0:T(1024)(128)(4,1)S(1)}, s32[]{:S(2)}) async-start(s8[4718592]{0:T(1024)(128)(4,1)} %bitcast.797), calls=%async_computation.6 | async-start | bytes 8388608
  306.6 13.7 copy-start.11
  308.3 43.1 %collective-permute-start.3 = (bf16[1,196,768]{2,1,0:T(8,128)(2,1)}, bf16[1,196,768]{2,1,0:T(8,128)(2,1)}, u32[]{:S(2)}, u32[]{:S(2)}) collective-permute-start(bf16[1,196,768]{2,1,0:T(8,128)(2,1)} %get-tuple-element.141), channel_id=1, source_target_pairs={{16,0},{17,1},{18,2},{19,3},{20,4},{21,5},{22,6},{23,7},{24,8},{25... | collective-permute-start | bytes 903176 | tf_op jit(solution)/shard_map/ppermute | solution.py:18
  309.6 10.7 copy-start.99
  310.5 9.9 copy-start.129
  310.5 9.9 copy-start.50
  310.5 9.9 copy-start.62
  310.5 14.9 %slice-start.6 = ((s8[4718592]{0:T(1024)(128)(4,1)}), s8[524288]{0:T(1024)(128)(4,1)S(1)}, s32[]{:S(2)}) async-start(s8[4718592]{0:T(1024)(128)(4,1)} %bitcast.797), calls=%async_computation.7 | async-start | bytes 1048576
  343.0 8.5 copy-start.26
  343.0 8.5 copy-start.74
  343.0 8.5 copy-start.93
  343.0 10.3 copy-start.158
  353.3 6.0 copy-start.59
  353.3 6.0 copy-start.12
  353.3 6.0 copy-start.100
  353.3 6.0 copy-start.130
  446.0 6.4 copy-start.15
  446.0 6.4 copy-start.16
  446.0 6.4 copy-start.33
  446.0 6.4 copy-start.52
  459.9 8.6 copy-start.101
  545.4 36.6 %copy-start.94 = (f32[1,196]{1,0:T(1,128)S(1)}, f32[1,196]{1,0:T(1,128)}, u32[]{:S(2)}) copy-start(f32[1,196]{1,0:T(1,128)} %get-tuple-element.159) | copy-start | bytes 2356
  582.0 12.1 copy-start.80
  614.8 10.9 slice-start
  618.2 7.9 slice-start.1
  618.2 8.5 slice-start.2
  (111 other events, 325.2 us)
Sparse Core Ops, SparseCore 0:
  636.6 739.3 all-reduce.5
where the time goes:
time: 1430 us
  waiting for transfers between devices  731 us (51%)
  local copies, waits for them, and re-layouts  324 us (23%)
  matrix products  284 us (20%)
  other arithmetic  63.1 us (4%)
  between operations  16 us (1%)
    unnamed x2, waiting for transfers between devices  731 us
    reshape x8, local copies, waits for them, and re-layouts, pack_grads(): item.reshape(leading, parts, -1).transpose(1, 0, 2).reshape(parts, -1)  106 us
    dot_general x18, matrix products, project(): jnp.einsum('bpd,de->bpe', left, right, preferred_element_type=jnp.float32)  84.4 us
    dot_general x12, matrix products, outer_rows(): jnp.einsum('bpd,bpe->de', left, right, preferred_element_type=jnp.float32)  76.3 us
    unnamed x366, local copies, waits for them, and re-layouts  65.9 us
    dot_general x12, matrix products, project_back(): jnp.einsum('bpe,de->bpd', left, right, preferred_element_type=jnp.float32)  40.1 us
  transfers between devices with their start and end apart: 5, of which 1 were waited for; matrix products, arithmetic and copies ran while one was open for 7% of the time, Pallas kernels for 0%

commit v1 on v0

v1 whole, which is shorter than its diff:
```python
import functools

import jax
import jax.numpy as jnp
from jax import lax
from jax.experimental import pallas as pl
from jax.experimental.pallas import tpu as pltpu
from jax.sharding import PartitionSpec as P

HEADS = 12
HEAD_DIM = 64
PAIRS = HEADS // 2
LANES = 2 * HEAD_DIM
MASK_LO = 59
MASK_HI = 117
TILE = 768
MIB = 2**20

epsilon = 1e-06
f32 = jnp.float32
bf16 = jnp.bfloat16
ANY = pl.BlockSpec(memory_space=pl.ANY)
SMEM = pl.BlockSpec(memory_space=pltpu.SMEM)
VMEM = pl.BlockSpec(memory_space=pltpu.VMEM)


def up16(count):
    return -(-count // 16) * 16


class Rows:
    def __init__(self, first, images, patches):
        most = patches - MASK_LO if first else MASK_HI
        self.first = first
        self.images = images
        self.patches = patches
        self.top = up16(most)
        self.rest = 0 if first else up16(patches - self.top)
        self.keys = self.top + self.rest
        self.queries = images * self.top
        self.total = images * self.keys


def dot(left, right):
    return jnp.dot(left, right, preferred_element_type=f32)


def dot_nt(left, right):
    return lax.dot_general(left, right, (((1,), (1,)), ((), ())), preferred_element_type=f32)


def dot_tn(left, right):
    return lax.dot_general(left, right, (((0,), (0,)), ((), ())), preferred_element_type=f32)


def iota(shape, dim):
    return lax.broadcasted_iota(jnp.int32, shape, dim)


def sort_rows(mask_ref, rows):
    masked = mask_ref[...].astype(f32)
    flag = 1.0 - masked if rows.first else masked
    n = rows.patches
    tri = jnp.where(iota((n, n), 0) <= iota((n, n), 1), 1.0, 0.0).astype(bf16)
    upto = dot(flag.astype(bf16), tri)
    count = jnp.sum(flag, axis=1, keepdims=True)
    at = iota(flag.shape, 1).astype(f32)
    place = jnp.where(flag > 0, upto - 1.0, count + at - upto)
    return flag, place, count


def pick(place, image, start, length):
    slots = iota((length, place.shape[1]), 0).astype(f32) + float(start)
    return jnp.where(slots == place[image : image + 1, :], 1.0, 0.0)


def valid_rows(count, rows):
    parts = [
        jnp.where(iota((rows.top, 1), 0).astype(f32) < count[b : b + 1, :], 1.0, 0.0)
        for b in range(rows.images)
    ]
    return jnp.concatenate(parts, axis=0)


def normed(states):
    centre = states - jnp.mean(states, axis=-1, keepdims=True)
    spread = jnp.mean(centre * centre, axis=-1, keepdims=True)
    scale = lax.rsqrt(spread + epsilon)
    return centre * scale, scale


def norm_back(grad, unit, scale, gain):
    inner = grad * gain
    along = jnp.mean(inner * unit, axis=-1, keepdims=True)
    return scale * (inner - jnp.mean(inner, axis=-1, keepdims=True) - unit * along)


def gelu_parts(values):
    size = jnp.abs(values) * (0.5**0.5)
    t = 1.0 / (1.0 + 0.3275911 * size)
    series = t * (
        0.254829592
        + t * (-0.284496736 + t * (1.421413741 + t * (-1.453152027 + t * 1.061405429)))
    )
    decay = jnp.exp(-0.5 * values * values)
    upper = 0.5 * series * decay
    below = jnp.where(values < 0, upper, 1.0 - upper)
    return below, decay * 0.3989422804014327


def total(values):
    return jnp.sum(values, axis=0, keepdims=True)


def key_rows(ref, image, lanes, rows):
    block = ref[image * rows.top : (image + 1) * rows.top, lanes]
    if rows.rest == 0:
        return block
    start = rows.queries + image * rows.rest
    return jnp.concatenate([block, ref[start : start + rows.rest, lanes]], axis=0)


class Copies:
    def __init__(self, sems):
        self.sems = sems
        self.used = 0

    def start(self, source, target):
        copy = pltpu.make_async_copy(source, target, self.sems.at[self.used])
        self.used += 1
        copy.start()
        return copy


SAVED = ("xs", "h1", "qkv", "p", "o", "a", "x1", "h2", "gp", "gl", "y")


def saved_shapes(rows, width, hidden):
    return {
        "xs": ((rows.total, width), bf16),
        "h1": ((rows.total, width), bf16),
        "qkv": ((rows.total, 3 * width), bf16),
        "p": ((rows.images * HEADS, rows.top, rows.keys), bf16),
        "o": ((rows.queries, width), bf16),
        "a": ((rows.queries, width), bf16),
        "x1": ((rows.queries, width), f32),
        "h2": ((rows.queries, width), bf16),
        "gp": ((rows.queries, hidden), bf16),
        "gl": ((rows.queries, hidden), bf16),
        "y": ((rows.queries, width), bf16),
    }


def forward_kernel(rows, n_in, *refs):
    (where_ref, mask_ref, tok_ref, lat_ref, gains_ref, biases_ref, upb_ref, downb_ref) = refs[:8]
    w_in, w_out, w_up, w_down = refs[8:12]
    result = refs[n_in]
    saved = dict(zip(SAVED, refs[n_in + 1 : n_in + 1 + len(SAVED)]))
    scratch = refs[n_in + 1 + len(SAVED) :]
    wi, wo, wu, wd = scratch[:4]
    held = dict(zip(SAVED, scratch[4 : 4 + len(SAVED)]))
    res, sems = scratch[4 + len(SAVED) :]
    width = wo.shape[0]
    images, top, queries = rows.images, rows.top, rows.queries
    scale = HEAD_DIM**-0.5

    @pl.when(where_ref[0] == (0 if rows.first else 1))
    def _():
        copies = Copies(sems)
        get_in = copies.start(w_in.at[0], wi)
        get_out = copies.start(w_out.at[0], wo)
        get_up = copies.start(w_up.at[0], wu)
        get_down = copies.start(w_down.at[0], wd)
        puts = []

        def put(name):
            puts.append(copies.start(held[name], saved[name]))

        flag, place, count = sort_rows(mask_ref, rows)

        def states_of(b, start, length):
            chosen = pick(place, b, start, length)
            if rows.first:
                return dot(chosen.astype(bf16), tok_ref[b])
            from_tokens = (chosen * flag[b : b + 1, :]).astype(bf16)
            from_latent = (chosen * (1.0 - flag[b : b + 1, :])).astype(bf16)
            return dot(from_tokens, tok_ref[b]) + dot(from_latent, lat_ref[b])

        pieces = [states_of(b, 0, top) for b in range(images)]
        if rows.rest:
            pieces += [states_of(b, top, rows.rest) for b in range(images)]
        states = jnp.concatenate(pieces, axis=0)
        held["xs"][...] = states.astype(bf16)
        put("xs")
        unit, _ = normed(states)
        h1 = (unit * gains_ref[0, 0:1, :] + biases_ref[0, 0:1, :]).astype(bf16)
        held["h1"][...] = h1
        put("h1")
        qkv = held["qkv"]
        get_in.wait()
        qkv[0:queries, 0:width] = (dot(h1[:queries], wi[:, :width]) + biases_ref[0, 1:2, :]).astype(
            bf16
        )
        if rows.rest:
            qkv[queries:, 0:width] = jnp.zeros((rows.total - queries, width), bf16)
        qkv[:, width : 2 * width] = dot(h1, wi[:, width : 2 * width]).astype(bf16)
        qkv[:, 2 * width :] = (dot(h1, wi[:, 2 * width :]) + biases_ref[0, 2:3, :]).astype(bf16)
        put("qkv")
        lane = iota((1, LANES), 1)
        sides = [(lane < HEAD_DIM), (lane >= HEAD_DIM)]
        masks = [jnp.where(side, 1.0, 0.0).astype(bf16) for side in sides]

        @pl.loop(0, PAIRS)
        def _(pair):
            lo = pl.multiple_of(pair * LANES, LANES)
            for b in range(images):
                q = qkv[b * top : (b + 1) * top, pl.ds(lo, LANES)]
                k = key_rows(qkv, b, pl.ds(width + lo, LANES), rows)
                v = key_rows(qkv, b, pl.ds(2 * width + lo, LANES), rows)
                at = iota((1, rows.keys), 1).astype(f32)
                if rows.first:
                    usable = at < count[b : b + 1, :]
                else:
                    usable = at < float(rows.patches)
                mixed = []
                for side in range(2):
                    raw = dot_nt(q * masks[side], k)
                    logits = jnp.where(usable, raw * scale, -1e30)
                    grown = jnp.exp(logits - jnp.max(logits, axis=-1, keepdims=True))
                    p = (grown * (1.0 / jnp.sum(grown, axis=-1, keepdims=True))).astype(bf16)
                    held["p"][(b * 2 + side) * PAIRS + pair] = p
                    mixed.append(dot(p, v))
                held["o"][b * top : (b + 1) * top, pl.ds(lo, LANES)] = jnp.where(
                    sides[0], mixed[0], mixed[1]
                ).astype(bf16)

        put("p")
        put("o")
        get_out.wait()
        a = dot(held["o"][...], wo[...]) + biases_ref[0, 3:4, :]
        held["a"][...] = a.astype(bf16)
        put("a")
        usable_rows = valid_rows(count, rows)
        x1 = states[:queries] + gains_ref[0, 1:2, :] * a * usable_rows
        held["x1"][...] = x1
        put("x1")
        unit, _ = normed(x1)
        h2 = (unit * gains_ref[0, 2:3, :] + biases_ref[0, 4:5, :]).astype(bf16)
        held["h2"][...] = h2
        put("h2")
        get_up.wait()
        get_down.wait()
        y = jnp.zeros((queries, width), f32)
        for start in range(0, wu.shape[1], TILE):
            cols = slice(start, start + TILE)
            u = dot(h2, wu[:, cols]) + upb_ref[:, cols]
            below, density = gelu_parts(u)
            gl = (u * below).astype(bf16)
            held["gl"][:, cols] = gl
            held["gp"][:, cols] = (below + u * density).astype(bf16)
            y = y + dot(gl, wd[cols, :])
        put("gl")
        put("gp")
        y = y + downb_ref[...]
        held["y"][...] = y.astype(bf16)
        put("y")
        x2 = (x1 + gains_ref[0, 3:4, :] * y * usable_rows).astype(bf16)
        for b in range(images):
            chosen = (pick(place, b, 0, top) * flag[b : b + 1, :]).astype(bf16)
            res[b] = dot_tn(chosen, x2[b * top : (b + 1) * top]).astype(bf16)
        puts.append(copies.start(res, result.at[0]))
        for copy in puts:
            copy.wait()


def forward(rows, where, mask, tokens, latent, weights, before):
    w_in, w_out, w_up, w_down, gains, biases, up_bias, down_bias = weights
    width, hidden = w_up.shape[1:]
    shapes = saved_shapes(rows, width, hidden)
    operands = [where, mask, tokens, latent, gains, biases, up_bias, down_bias]
    operands += [w_in, w_out, w_up, w_down]
    in_specs = [SMEM] + [VMEM] * 7 + [ANY] * 4
    aliases = {}
    if before is not None:
        aliases[len(operands)] = 0
        operands.append(before)
        in_specs.append(ANY)
    outs = [jax.ShapeDtypeStruct((1,) + tokens.shape, bf16)]
    outs += [jax.ShapeDtypeStruct(*shapes[name]) for name in SAVED]
    results = pl.pallas_call(
        functools.partial(forward_kernel, rows, len(operands)),
        out_shape=outs,
        in_specs=in_specs,
        out_specs=[ANY] * len(outs),
        scratch_shapes=[pltpu.VMEM(w.shape[1:], bf16) for w in (w_in, w_out, w_up, w_down)]
        + [pltpu.VMEM(*shapes[name]) for name in SAVED]
        + [pltpu.VMEM(tokens.shape, bf16), pltpu.SemaphoreType.DMA((20,))],
        input_output_aliases=aliases,
        compiler_params=pltpu.CompilerParams(vmem_limit_bytes=52 * MIB),
        cost_estimate=pl.CostEstimate(
            flops=2 * rows.queries * 12 * width * width,
            bytes_accessed=12 * 2 * width * width,
            transcendentals=0,
        ),
        name="forward_first" if rows.first else "forward_second",
    )(*operands)
    return results[0], dict(zip(SAVED, results[1:]))


def split_store(bit, keep, send, tile, shards, base, order):
    height = tile.shape[0] // shards
    for own in range(2):

        @pl.when(bit == own)
        def _():
            for d in range(shards):
                x, y, z = d & 1, (d >> 1) & 1, d >> 2
                mine, slot = (x, 2 * z + y) if order == 0 else (y, 2 * z + x)
                target = keep if mine == own else send
                target[slot - base] = tile[d * height : (d + 1) * height]


def bit_of(where_ref, order):
    return (where_ref[1] >> order) & 1


def down_kernel(rows, order, *refs):
    where_ref, mask_ref, cot_ref, ret_ref, gains_ref, y_ref, gl_ref = refs[:7]
    outs = refs[7:-1]
    if order is None:
        plain, g_out, dy_out, vec = outs
    else:
        keep, send, g_out, dy_out, vec = outs
    turned = refs[-1]
    images, top = rows.images, rows.top

    @pl.when(where_ref[0] == (0 if rows.first else 1))
    def _():
        @pl.when(pl.program_id(0) == 0)
        def _():
            flag, place, count = sort_rows(mask_ref, rows)
            pieces = []
            for b in range(images):
                chosen = (pick(place, b, 0, top) * flag[b : b + 1, :]).astype(bf16)
                piece = dot(chosen, cot_ref[0, b])
                if rows.first:
                    piece = piece + dot(chosen, ret_ref[b])
                pieces.append(piece)
            grad = jnp.concatenate(pieces, axis=0)
            g_out[...] = grad
            dy = (grad * gains_ref[0, 3:4, :] * valid_rows(count, rows)).astype(bf16)
            dy_out[...] = dy
            vec[...] = jnp.zeros(vec.shape, f32)
            vec[0:1, :] = total(grad * y_ref[...].astype(f32))
            vec[1:2, :] = total(dy.astype(f32))
            turned[...] = dy.T

        tile = dot(turned[...], gl_ref[...]).astype(bf16)
        if order is None:
            plain[...] = tile
        else:
            split_store(bit_of(where_ref, order), keep, send, tile, 16, 0, order)


def grad_outs(order, shards, full, block, index):
    if order is None:
        return [jax.ShapeDtypeStruct(full, bf16)], [pl.BlockSpec(block, index)]
    return [jax.ShapeDtypeStruct(shards, bf16)] * 2, None


def whole(shape):
    return pl.BlockSpec(shape, lambda *_: (0,) * len(shape))


def down_back(rows, order, where, mask, cot, returned, gains, saved):
    queries, width = saved["y"].shape
    hidden = saved["gl"].shape[1]
    if order is None:
        grads = [jax.ShapeDtypeStruct((width, hidden), bf16)]
        specs = [pl.BlockSpec((width, TILE), lambda t: (0, t))]
    else:
        grads = [jax.ShapeDtypeStruct((8, width // 16, hidden), bf16)] * 2
        specs = [pl.BlockSpec((8, width // 16, TILE), lambda t: (0, 0, t))] * 2
    vectors = [
        jax.ShapeDtypeStruct((queries, width), f32),
        jax.ShapeDtypeStruct((queries, width), bf16),
        jax.ShapeDtypeStruct((8, width), f32),
    ]
    return pl.pallas_call(
        functools.partial(down_kernel, rows, order),
        grid=(hidden // TILE,),
        out_shape=grads + vectors,
        in_specs=[SMEM]
        + [whole(a.shape) for a in (mask, cot, returned, gains, saved["y"])]
        + [pl.BlockSpec((queries, TILE), lambda t: (0, t))],
        out_specs=specs + [whole(v.shape) for v in vectors],
        scratch_shapes=[pltpu.VMEM((width, queries), bf16)],
        compiler_params=pltpu.CompilerParams(vmem_limit_bytes=40 * MIB),
        cost_estimate=pl.CostEstimate(
            flops=2 * queries * hidden * width, bytes_accessed=4 * hidden * width, transcendentals=0
        ),
        name="down_grad",
    )(where, mask, cot, returned, gains, saved["y"], saved["gl"])


def up_kernel(rows, order, *refs):
    where_ref, dy_ref, gp_ref, h2_ref, down_ref, up_ref = refs[:6]
    if order is None:
        plain, upb_out, dh2_out = refs[6:]
    else:
        keep, send, upb_out, dh2_out = refs[6:]
    step = pl.program_id(0)

    @pl.when(where_ref[0] == (0 if rows.first else 1))
    def _():
        dgl = dot_nt(dy_ref[...], down_ref[0])
        du = (dgl * gp_ref[...].astype(f32)).astype(bf16)
        upb_out[...] = total(du.astype(f32))
        tile = dot_tn(du, h2_ref[...]).astype(bf16)
        if order is None:
            plain[...] = tile
        else:
            split_store(bit_of(where_ref, order), keep, send, tile, 4, 0, order)
        part = dot_nt(du, up_ref[0])

        @pl.when(step == 0)
        def _():
            dh2_out[...] = part

        @pl.when(step > 0)
        def _():
            dh2_out[...] += part


def up_back(rows, order, where, dy, saved, w_down, w_up):
    queries, width = dy.shape
    hidden = w_up.shape[2]
    if order is None:
        grads = [jax.ShapeDtypeStruct((hidden, width), bf16)]
        specs = [pl.BlockSpec((TILE, width), lambda t: (t, 0))]
    else:
        grads = [jax.ShapeDtypeStruct((8, hidden // 16, width), bf16)] * 2
        specs = [pl.BlockSpec((2, hidden // 16, width), lambda t: (t, 0, 0))] * 2
    vectors = [
        jax.ShapeDtypeStruct((1, hidden), f32),
        jax.ShapeDtypeStruct((queries, width), f32),
    ]
    return pl.pallas_call(
        functools.partial(up_kernel, rows, order),
        grid=(hidden // TILE,),
        out_shape=grads + vectors,
        in_specs=[
            SMEM,
            whole(dy.shape),
            pl.BlockSpec((queries, TILE), lambda t: (0, t)),
            whole(dy.shape),
            pl.BlockSpec((1, TILE, width), lambda t: (0, t, 0)),
            pl.BlockSpec((1, width, TILE), lambda t: (0, 0, t)),
        ],
        out_specs=specs + [pl.BlockSpec((1, TILE), lambda t: (0, t)), whole((queries, width))],
        compiler_params=pltpu.CompilerParams(vmem_limit_bytes=40 * MIB),
        cost_estimate=pl.CostEstimate(
            flops=6 * queries * hidden * width, bytes_accessed=6 * hidden * width, transcendentals=0
        ),
        name="up_grad",
    )(where, dy, saved["gp"], saved["h2"], w_down, w_up)


ATTEND = ("dh2", "x1", "g", "a", "o", "w_out", "qkv", "p", "w_in", "xs")


def attend_kernel(rows, order, n_in, n_out, *refs):
    where_ref, mask_ref, gains_ref, biases_ref, vec_ref, upb_ref = refs[:6]
    source = dict(zip(ATTEND, refs[6:16]))
    outs = refs[n_in : n_in + n_out]
    dqkv_out, token_out, ret_out, vec_out = outs[-4:]
    scratch = refs[n_in + n_out :]
    held = dict(zip(ATTEND, scratch[: len(ATTEND)]))
    dqkv, tok_buf, ret_buf, vec_buf = scratch[len(ATTEND) : len(ATTEND) + 4]
    halves = scratch[len(ATTEND) + 4 : -1]
    sems = scratch[-1]
    images, top, queries = rows.images, rows.top, rows.queries
    width = held["w_out"].shape[0]
    scale = HEAD_DIM**-0.5

    @pl.when(where_ref[0] == (0 if rows.first else 1))
    def _():
        copies = Copies(sems)
        gets = {}
        for name in ATTEND:
            ref = source[name]
            gets[name] = copies.start(ref.at[0] if name in ("w_in", "w_out") else ref, held[name])
        puts = []
        flag, place, count = sort_rows(mask_ref, rows)
        usable_rows = valid_rows(count, rows)
        for name in ("dh2", "x1", "g"):
            gets[name].wait()
        unit, spread = normed(held["x1"][...])
        dh2 = held["dh2"][...]
        gain_two = total(dh2 * unit)
        bias_two = total(dh2)
        dx1 = held["g"][...] + norm_back(dh2, unit, spread, gains_ref[0, 2:3, :])
        da = (dx1 * gains_ref[0, 1:2, :] * usable_rows).astype(bf16)
        for name in ("a", "o", "w_out"):
            gets[name].wait()
        scale_one = total(dx1 * held["a"][...].astype(f32) * usable_rows)
        out_bias = total(da.astype(f32))
        tile = dot_tn(da, held["o"][...]).astype(bf16)
        if order is None:
            halves[0][...] = tile
        else:
            split_store(bit_of(where_ref, order), halves[0], halves[1], tile, 16, 0, order)
        for half, out in zip(halves, outs):
            puts.append(copies.start(half, out))
        do_ref = held["o"]
        do_ref[...] = dot_nt(da, held["w_out"][...]).astype(bf16)
        for name in ("qkv", "p"):
            gets[name].wait()
        qkv = held["qkv"]
        lane = iota((1, LANES), 1)
        sides = [(lane < HEAD_DIM), (lane >= HEAD_DIM)]
        masks = [jnp.where(side, 1.0, 0.0).astype(bf16) for side in sides]
        if rows.rest:
            dqkv[queries:, 0:width] = jnp.zeros((rows.total - queries, width), bf16)

        @pl.loop(0, PAIRS)
        def _(pair):
            lo = pl.multiple_of(pair * LANES, LANES)
            for b in range(images):
                q = qkv[b * top : (b + 1) * top, pl.ds(lo, LANES)]
                k = key_rows(qkv, b, pl.ds(width + lo, LANES), rows)
                v = key_rows(qkv, b, pl.ds(2 * width + lo, LANES), rows)
                do = do_ref[b * top : (b + 1) * top, pl.ds(lo, LANES)]
                parts = []
                for side in range(2):
                    p = held["p"][(b * 2 + side) * PAIRS + pair]
                    wide = p.astype(f32)
                    dp = dot_nt(do * masks[side], v)
                    inner = jnp.sum(wide * dp, axis=-1, keepdims=True)
                    draw = (wide * (dp - inner) * scale).astype(bf16)
                    parts.append((dot(draw, k), dot_tn(draw, q), dot_tn(p, do)))
                for at in range(3):
                    merged = jnp.where(sides[0], parts[0][at], parts[1][at]).astype(bf16)
                    lanes = pl.ds(at * width + lo, LANES)
                    dqkv[b * top : (b + 1) * top, lanes] = merged[:top]
                    if rows.rest and at > 0:
                        start = queries + b * rows.rest
                        dqkv[start : start + rows.rest, lanes] = merged[top:]

        puts.append(copies.start(dqkv, dqkv_out))
        gets["w_in"].wait()
        gets["xs"].wait()
        dh1 = jnp.zeros((rows.total, width), f32)
        for at in range(3):
            cols = slice(at * width, (at + 1) * width)
            dh1 = dh1 + dot_nt(dqkv[:, cols], held["w_in"][:, cols])
        unit, spread = normed(held["xs"][...].astype(f32))
        dx = norm_back(dh1, unit, spread, gains_ref[0, 0:1, :])
        if rows.rest:
            rest = dx[queries:]
        dx = dx[:queries] + dx1
        high = dx.astype(bf16)
        low = (dx - high.astype(f32)).astype(bf16)
        for b in range(images):
            chosen = pick(place, b, 0, top)
            mine = (chosen * flag[b : b + 1, :]).astype(bf16)
            part = slice(b * top, (b + 1) * top)
            tok_buf[b] = dot_tn(mine, high[part]) + dot_tn(mine, low[part])
            if not rows.first:
                other = (chosen * (1.0 - flag[b : b + 1, :])).astype(bf16)
                back = dot_tn(other, high[part])
                tail = pick(place, b, top, rows.rest).astype(bf16)
                part = slice(b * rows.rest, (b + 1) * rows.rest)
                back = back + dot_tn(tail, rest[part].astype(bf16))
                ret_buf[b] = back.astype(bf16)
        puts.append(copies.start(tok_buf, token_out.at[0]))
        if not rows.first:
            puts.append(copies.start(ret_buf, ret_out))
        vec_buf[...] = jnp.zeros(vec_buf.shape, f32)
        vec_buf[0:1, :] = total(dh1 * unit)
        vec_buf[1:2, :] = scale_one
        vec_buf[2:3, :] = gain_two
        vec_buf[3:4, :] = vec_ref[0:1, :]
        vec_buf[4:5, :] = total(dh1)
        vec_buf[5:6, :] = total(dqkv[:, 0:width].astype(f32))
        vec_buf[6:7, :] = total(dqkv[:, 2 * width :].astype(f32))
        vec_buf[7:8, :] = out_bias
        vec_buf[8:9, :] = bias_two
        vec_buf[9:10, :] = vec_ref[1:2, :]
        for at in range(upb_ref.shape[1] // width):
            vec_buf[10 + at : 11 + at, :] = upb_ref[:, at * width : (at + 1) * width]
        puts.append(copies.start(vec_buf, vec_out))
        for copy in puts:
            copy.wait()


def attend_back(rows, order, where, mask, weights, vec, upb, dh2, grad, saved, token_before):
    w_in, w_out, _, _, gains, biases, _, _ = weights
    queries, width = dh2.shape
    shape = (rows.images, rows.patches, width)
    values = dict(saved, dh2=dh2, g=grad, w_in=w_in, w_out=w_out)
    operands = [where, mask, gains, biases, vec, upb] + [values[name] for name in ATTEND]
    in_specs = [SMEM] + [VMEM] * 5 + [ANY] * len(ATTEND)
    if order is None:
        grads = [jax.ShapeDtypeStruct((width, width), bf16)]
    else:
        grads = [jax.ShapeDtypeStruct((8, width // 16, width), bf16)] * 2
    outs = grads + [
        jax.ShapeDtypeStruct((rows.total, 3 * width), bf16),
        jax.ShapeDtypeStruct((1,) + shape, f32),
        jax.ShapeDtypeStruct(shape, bf16),
        jax.ShapeDtypeStruct((16, width), f32),
    ]
    aliases = {}
    if token_before is not None:
        aliases[len(operands)] = len(grads) + 1
        operands.append(token_before)
        in_specs.append(ANY)
    held = [
        pltpu.VMEM(values[n].shape[1:] if n in ("w_in", "w_out") else values[n].shape, values[n].dtype)
        for n in ATTEND
    ]
    return pl.pallas_call(
        functools.partial(attend_kernel, rows, order, len(operands), len(outs)),
        out_shape=outs,
        in_specs=in_specs,
        out_specs=[ANY] * len(outs),
        scratch_shapes=held
        + [
            pltpu.VMEM((rows.total, 3 * width), bf16),
            pltpu.VMEM(shape, f32),
            pltpu.VMEM(shape, bf16),
            pltpu.VMEM((16, width), f32),
        ]
        + [pltpu.VMEM(g.shape, g.dtype) for g in grads]
        + [pltpu.SemaphoreType.DMA((20,))],
        input_output_aliases=aliases,
        compiler_params=pltpu.CompilerParams(vmem_limit_bytes=52 * MIB),
        cost_estimate=pl.CostEstimate(
            flops=2 * rows.total * 6 * width * width,
            bytes_accessed=16 * width * width,
            transcendentals=0,
        ),
        name="attend_back",
    )(*operands)


def in_kernel(rows, order, where_ref, dqkv_ref, h1_ref, *outs):
    @pl.when(where_ref[0] == (0 if rows.first else 1))
    def _():
        tile = dot_tn(dqkv_ref[...], h1_ref[...]).astype(bf16)
        if order is None:
            outs[0][...] = tile
        else:
            split_store(bit_of(where_ref, order), outs[0], outs[1], tile, 8, 0, order)


def in_back(rows, order, where, dqkv, h1):
    tall, wide = dqkv.shape
    width = h1.shape[1]
    half = wide // 2
    if order is None:
        grads = [jax.ShapeDtypeStruct((wide, width), bf16)]
        specs = [pl.BlockSpec((half, width), lambda t: (t, 0))]
    else:
        grads = [jax.ShapeDtypeStruct((8, wide // 16, width), bf16)] * 2
        specs = [pl.BlockSpec((4, wide // 16, width), lambda t: (t, 0, 0))] * 2
    return pl.pallas_call(
        functools.partial(in_kernel, rows, order),
        grid=(2,),
        out_shape=grads,
        in_specs=[SMEM, pl.BlockSpec((tall, half), lambda t: (0, t)), whole(h1.shape)],
        out_specs=specs,
        compiler_params=pltpu.CompilerParams(vmem_limit_bytes=40 * MIB),
        cost_estimate=pl.CostEstimate(
            flops=2 * tall * wide * width, bytes_accessed=4 * wide * width, transcendentals=0
        ),
        name="in_grad",
    )(where, dqkv, h1)


def wide_sum(*terms):
    result = terms[0].astype(f32)
    for term in terms[1:]:
        result = result + term.astype(f32)
    return result


def swap(value, by, count):
    return lax.ppermute(value, "dp", [(i, i ^ by) for i in range(count)])


def line_sum(parts, z, stride, count):
    length = parts.shape[0]
    right = left = None

    def part(at):
        return lax.dynamic_index_in_dim(parts, jnp.clip(at, 0, length - 1), 0, keepdims=False)

    for t in range(length - 1):
        ahead = length - 1 - t
        to_right, to_left = part(z + ahead), part(z - ahead)
        if t > 0:
            to_right = wide_sum(to_right, right).astype(bf16)
            to_left = wide_sum(to_left, left).astype(bf16)
        pairs = [
            (i, i + stride)
            for i in range(count)
            if i // stride % length <= t and i // stride % length < length - 1
        ]
        back = [(count - 1 - i, count - 1 - j) for i, j in pairs]
        right = lax.ppermute(to_right, "dp", pairs)
        left = lax.ppermute(to_left, "dp", back)
    return wide_sum(part(z), right, left)


def half_of(parts, bit, axis):
    keep = lax.dynamic_index_in_dim(parts, bit, axis, keepdims=False)
    send = lax.dynamic_index_in_dim(parts, 1 - bit, axis, keepdims=False)
    return keep, send


def on_device(
    tokens,
    patch_mask,
    cotangent,
    in_weight,
    out_weight,
    up_weight,
    down_weight,
    gains,
    biases,
    up_bias,
    down_bias,
):
    weights = (in_weight, out_weight, up_weight, down_weight, gains, biases, up_bias, down_bias)
    images, patches, width = tokens.shape
    hidden = up_weight.shape[2]
    count = lax.axis_size("dp")
    section = lax.axis_index("section")
    place = lax.axis_index("dp")
    is_first = section == 0
    where = jnp.stack([section, place]).astype(jnp.int32)
    small = count == 16
    orders = {"down": 0, "up": 1, "out": 0, "in": 1} if small else dict.fromkeys(
        ("down", "up", "out", "in")
    )
    rows = [Rows(True, images, patches), Rows(False, images, patches)]

    result, kept_first = forward(rows[0], where, patch_mask, tokens, tokens, weights, None)
    latent = lax.ppermute(result[0], "section", [(0, 1)])
    result, kept_second = forward(rows[1], where, patch_mask, tokens, latent, weights, result)
    kept = [kept_first, kept_second]

    grads = [None, None]
    vectors = [None, None]
    returned = latent
    token_grads = None
    for phase in (1, 0):
        layout, saved = rows[phase], kept[phase]
        pairs = [(phase * count + i, phase * count + (i ^ 1)) for i in range(count)]
        cross = [(phase * count + i, phase * count + (i ^ 2)) for i in range(count)]

        def first_exchange(halves, order):
            if order is None:
                return halves
            keep, send = halves
            got = lax.ppermute(send, ("section", "dp"), cross if order else pairs)
            return [keep, got]

        *halves, grad, dy, vec = down_back(
            layout, orders["down"], where, patch_mask, cotangent, returned, gains, saved
        )
        mine = {"down": first_exchange(halves, orders["down"])}
        *halves, upb, dh2 = up_back(
            layout, orders["up"], where, dy, saved, down_weight, up_weight
        )
        mine["up"] = first_exchange(halves, orders["up"])
        *halves, dqkv, token_grads, back, vec = attend_back(
            layout, orders["out"], where, patch_mask, weights, vec, upb, dh2, grad, saved, token_grads
        )
        if phase == 1:
            returned = lax.ppermute(back, "section", [(1, 0)])
        mine["out"] = first_exchange(halves, orders["out"])
        halves = in_back(layout, orders["in"], where, dqkv, saved["h1"])
        mine["in"] = first_exchange(halves, orders["in"])
        grads[phase] = mine
        vectors[phase] = vec

    vec = jnp.where(is_first, vectors[0], vectors[1])
    finals = {}
    if small:
        x, y, z = place & 1, (place >> 1) & 1, place >> 2
        for name in ("down", "up", "out", "in"):
            merged = jnp.where(
                is_first, wide_sum(*grads[0][name]), wide_sum(*grads[1][name])
            ).astype(bf16)
            first = orders[name]
            second_bit, step = (y, 2) if first == 0 else (x, 1)
            shape = merged.shape[1:]
            merged = merged.reshape((4, 2) + shape)
            if name in ("down", "up"):
                part = line_sum(merged, z, 4, count).astype(bf16)
                keep, send = half_of(part, second_bit, 0)
                finals[name] = wide_sum(keep, swap(send, step, count))
            else:
                keep, send = half_of(merged, second_bit, 1)
                part = wide_sum(keep, swap(send, step, count)).astype(bf16)
                finals[name] = line_sum(part, z, 4, count)
        for by in (1, 2, 4, 8):
            vec = vec + swap(vec, by, count)
    else:
        for name in ("down", "up", "out", "in"):
            merged = jnp.where(is_first, grads[0][name][0], grads[1][name][0])
            finals[name] = lax.psum_scatter(
                merged.astype(f32), "dp", scatter_dimension=0, tiled=True
            )
        vec = lax.psum(vec, "dp")

    def columns(values):
        size = values.shape[-1] // count
        return lax.dynamic_slice_in_dim(values, place * size, size, values.ndim - 1)

    return (
        result,
        token_grads,
        finals["in"].T[None],
        finals["out"].T[None],
        finals["up"].T[None],
        finals["down"].T[None],
        columns(vec[0:4])[None],
        columns(vec[4:9])[None],
        columns(vec[10:14].reshape(1, hidden)),
        columns(vec[9:10]),
    )


def solution(mesh):
    return jax.shard_map(
        on_device,
        mesh=mesh,
        in_specs=(
            P("dp", None, None),
            P("dp", None),
            P("section", "dp", None, None),
            P("section", None, None),
            P("section", None, None),
            P("section", None, None),
            P("section", None, None),
            P("section", None, None),
            P("section", None, None),
            P("section", None),
            P("section", None),
        ),
        out_specs=(
            P("section", "dp", None, None),
            P("section", "dp", None, None),
            P("section", None, "dp"),
            P("section", None, "dp"),
            P("section", None, "dp"),
            P("section", None, "dp"),
            P("section", None, "dp"),
            P("section", None, "dp"),
            P("section", "dp"),
            P("section", "dp"),
        ),
        check_vma=False,
    )
```

time: 1430 us -> 375 us (0.26)
  waiting for transfers between devices: 731 us -> 141 us
  local copies, waits for them, and re-layouts: 324 us -> 38.1 us
  matrix products: 284 us -> 0 us
  starting transfers between devices: 7.54 us -> 96.7 us
  Pallas kernels: 0 us -> 79.1 us
  other arithmetic: 63.1 us -> 16 us
    unnamed x2 -> x0, waiting for transfers between devices: 731 us -> none
    dot_general x59 -> x0, matrix products: 266 us -> none  [the longest x18 84.4 us: project(): jnp.einsum('bpd,de->bpe', left, right, preferred_element_type=jnp.float32)]
    ppermute x4 -> x42, waiting for transfers between devices: 0.01 us -> 141 us  [the longest x8 48.2 us: swap(): return lax.ppermute(value, 'dp', [(i, i ^ by) for i in range(count)])]
    reshape x14 -> x0, local copies, waits for them, and re-layouts: 117 us -> none  [the longest x8 106 us: pack_grads(): item.reshape(leading, parts, -1).transpose(1, 0, 2).reshape(parts, -1)]
    ppermute x4 -> x42, starting transfers between devices: 7.5 us -> 96.7 us  [the longest x12 51.5 us: line_sum(): right = lax.ppermute(to_right, 'dp', pairs)]
    pallas_call x0 -> x10, Pallas kernels: none -> 79.1 us  [the longest x2 33.1 us: forward(): pl.pallas_call(functools.partial(forward_kernel, rows, len(operands)), ou...]
    reduce_sum x36 -> x0, other arithmetic: 46.2 us -> none  [the longest x12 24.5 us: row_total(): return jnp.sum(values, axis=(0, 1))]
    another operation x31 -> x0, local copies, waits for them, and re-layouts: 38.7 us -> none  [the longest x18 22.4 us: backward_block(): jnp.stack([grad_bias_one, joined_total[:width], joined_total[2 * width:],...]
  transfers between devices with their start and end apart: 5 -> 42, of which waited for: 1 -> 14; matrix products, arithmetic and copies ran while one was open for 7% -> 6% of each run, Pallas kernels for 0% -> 11%
where the time goes in v1:
time: 375 us; the launch traced here: 373 us
  waiting for transfers between devices  141 us (38%)
  starting transfers between devices  96.7 us (26%)
  Pallas kernels  79.1 us (21%)
  local copies, waits for them, and re-layouts  38.1 us (10%)
  other arithmetic  16 us (4%)
    ppermute x12, starting transfers between devices, line_sum(): right = lax.ppermute(to_right, 'dp', pairs)  51.5 us
    ppermute x8, waiting for transfers between devices, swap(): return lax.ppermute(value, 'dp', [(i, i ^ by) for i in range(count)])  48.2 us
    ppermute x1, waiting for transfers between devices, on_device(): returned = lax.ppermute(back, 'section', [(1, 0)])  46.5 us
    pallas_call x2, Pallas kernels, forward(): pl.pallas_call(functools.partial(forward_kernel, rows, len(operands)), ou...  33.1 us
    unnamed x89, local copies, waits for them, and re-layouts  30.9 us
    ppermute x12, waiting for transfers between devices, line_sum(): right = lax.ppermute(to_right, 'dp', pairs)  28.6 us
    ppermute x8, starting transfers between devices, first_exchange(): got = lax.ppermute(send, ('section', 'dp'), cross if order else pairs)  22.5 us
    pallas_call x2, Pallas kernels, attend_back(): pl.pallas_call(functools.partial(attend_kernel, rows, order, len(operands...  18.8 us
  transfers between devices with their start and end apart: 42, of which 14 were waited for; matrix products, arithmetic and copies ran while one was open for 6% of the time, Pallas kernels for 11%

profile of v1, /device:TPU:0, one launch (start us, length us, event | category | flops | bytes accessed | tf_op | source)
XLA Modules:
  0.0 373.1 jit_solution(3936718561131451565)
XLA Ops:
  1.4 1.9 copy.40.refs_2_.refs_3_
  6.2 19.1 %forward_first.1 = (bf16[1,2,196,768]{3,2,1,0:T(8,128)(2,1)}, bf16[288,768]{1,0:T(8,128)(2,1)S(1)}, bf16[288,768]{1,0:T(8,128)(2,1)S(1)}, bf16[288,2304]{1,0:T(8...) custom-call(s32[2]{0:T(128)S(1)} %pad_add_fusion.refs_0_.where_ref, ...), custom_call_target="tpu_custom_call" | custom-call | flops 4076863488 | bytes 14155776 | tf_op jit(solution)/shard_map/forward_first/pallas_call | solution.py:290
  25.2 1.5 copy.39
  26.8 1.3 collective-permute-start
  28.2 1.5 collective-permute-done
  30.6 14.0 %forward_second.1 = (bf16[1,2,196,768]{3,2,1,0:T(8,128)(2,1)}, bf16[416,768]{1,0:T(8,128)(2,1)}, bf16[416,768]{1,0:T(8,128)(2,1)}, bf16[416,2304]{1,0:T(8,128)(2...) custom-call(s32[2]{0:T(128)S(1)} %pad_add_fusion.refs_0_.where_ref, ...), custom_call_target="tpu_custom_call", output_to_operand_aliasing={{0}: (12, {})} | custom-call | flops 3623878656 | bytes 14155776 | tf_op jit(solution)/shard_map/forward_second/pallas_call | solution.py:290
  45.4 1.4 copy-done.28
  48.9 1.4 copy-done.1
  50.3 1.5 copy-done.22
  51.8 3.4 up_grad.2
  56.1 1.4 copy-done.21
  58.6 1.7 copy.46
  60.3 1.3 collective-permute-start.1
  61.6 1.5 collective-permute-start.12
  63.1 46.5 %collective-permute-done.1 = bf16[2,196,768]{2,0,1:T(2,128)(2,1)S(1)} collective-permute-done((bf16[2,196,768]{2,0,1:T(2,128)(2,1)S(1)}, bf16[2,196,768]{2,0,1:T(2,128)(2,1)S(1)}, u32[]{:S(2)}, u32[]{:S(2)}) %collective-permute-start.1) | collective-permute-done | bytes 602144 | tf_op jit(solution)/shard_map/ppermute | solution.py:783
  109.8 6.0 %down_grad.3 = (bf16[8,48,3072]{2,1,0:T(8,128)(2,1)S(1)}, bf16[8,48,3072]{2,1,0:T(8,128)(2,1)}, f32[288,768]{1,0:T(8,128)S(1)}, bf16[288,768]{1,0:T(8,128)(2,1)S(1)}, f32[8,768]{1,0:T(8,128)S(1)}) custom-call(s32[2]{0:T(128)S(1)} %pad_add_fusion.refs_0_.where_ref, s32[2,196]{1,0:T(2,128)S(1)} %copy-done.18, bf16[1,2,196,768]{3,2,1,0:T(8,128)(2,1)S(1)} %copy.47.refs_2_, ...), custom_call_target="tpu_custom_call" | custom-call | flops 1358954496 | bytes 9437184 | tf_op jit(solution)/shard_map/down_grad/pallas_call | solution.py:389
  115.7 1.5 copy-done.5
  118.3 10.9 %up_grad.3 = (bf16[8,192,768]{2,1,0:T(8,128)(2,1)S(1)}, bf16[8,192,768]{2,1,0:T(8,128)(2,1)S(1)}, f32[1,3072]{1,0:T(1,128)S(1)}, f32[288,768]{1,0:T(8,128)S(1)}) custom-call(s32[2]{0:T(128)S(1)} %pad_add_fusion.refs_0_.where_ref, bf16[288,768]{1,0:T(8,128)(2,1)S(1)} %get-tuple-element.88.refs_1_, bf16[288,3072]{1,0:T(8,128)(2,1)S(1)} %copy-done.25, ...), custom_call_target="tpu_custom_call" | custom-call | flops 4076863488 | bytes 14155776 | tf_op jit(solution)/shard_map/up_grad/pallas_call | solution.py:448
  129.1 1.5 copy-done.3
  131.5 1.4 copy-done.23
  132.9 17.6 %attend_back.3 = (bf16[8,48,768]{2,1,0:T(8,128)(2,1)}, bf16[8,48,768]{2,1,0:T(8,128)(2,1)}, bf16[288,2304]{1,0:T(8,128)(2,1)}, f32[1,2,196,768]{3,2,1,0:T(8,128)...) custom-call(s32[2]{0:T(128)S(1)} %pad_add_fusion.refs_0_.where_ref, ...), custom_call_target="tpu_custom_call", output_to_operand_aliasing={{3}: (16, {})} | custom-call | flops 2038431744 | bytes 9437184 | tf_op jit(solution)/shard_map/attend_back/pallas_call | solution.py:623
  150.6 4.9 %collective-permute-start.11 = (bf16[8,48,768]{2,1,0:T(8,128)(2,1)}, bf16[8,48,768]{2,1,0:T(8,128)(2,1)}, u32[]{:S(2)}, u32[]{:S(2)}) collective-permute-start(bf16[8,48,768]{2,1,0:T(8,128)(2,1)} %get-tuple-element.111), channel_id=1, source_target_pairs={{0,1},{1,0},{2,3},{3,2},{4,5},{5,4},{6,7},{7,6},{8,9},{9,8},{10,11... | collective-permute-start | bytes 1769480 | tf_op jit(solution)/shard_map/ppermute | solution.py:768
  155.4 1.5 copy-done.24
  158.0 1.9 in_grad.3
  159.9 1.3 copy-done.7
  161.2 1.9 collective-permute-start.3
  163.1 7.8 %collective-permute-done.38 = f32[16,768]{1,0:T(8,128)S(1)} collective-permute-done((f32[16,768]{1,0:T(8,128)S(1)}, f32[16,768]{1,0:T(8,128)S(1)}, u32[]{:S(2)}, u32[]{:S(2)}) %collective-permute-start.38) | collective-permute-done | bytes 49184 | tf_op jit(solution)/shard_map/ppermute | solution.py:690
  170.9 2.1 collective-permute-start.39
  173.0 2.2 collective-permute-start.30
  175.3 2.4 collective-permute-start.40
  177.7 1.3 copy-done.29
  179.0 4.2 %in_grad.2 = (bf16[8,144,768]{2,1,0:T(8,128)(2,1)S(1)}, bf16[8,144,768]{2,1,0:T(8,128)(2,1)}) custom-call(s32[2]{0:T(128)S(1)} %pad_add_fusion.refs_0_.where_ref, bf16[288,2304]{1,0:T(8,128)(2,1)S(1)} %copy-done.29, bf16[288,768]{1,0:T(8,128)(2,1)S(1)} %get-tuple-element.103.h1_ref), custom_call_target="tpu_custom_call" | custom-call | flops 1019215872 | bytes 7077888 | tf_op jit(solution)/shard_map/in_grad/pallas_call | solution.py:668
  183.2 3.5 collective-permute-start.29
  186.8 3.5 collective-permute-start.2
  190.2 2.6 collective-permute-start.41
  192.9 1.5 select_convert_fusion.3
  196.0 2.4 copy.52
  198.5 3.1 copy.53
  201.6 33.5 %collective-permute-done.13 = bf16[4,48,768]{2,1,0:T(8,128)(2,1)S(1)} collective-permute-done((bf16[4,48,768]{2,1,0:T(8,128)(2,1)S(1)}, bf16[4,48,768]{2,1,0:T(8,128)(2,1)S(1)}, u32[]{:S(2)}, u32[]{:S(2)}) %collective-permute-start.13) | collective-permute-done | bytes 294944 | tf_op jit(solution)/shard_map/ppermute | solution.py:690
  235.2 1.3 collective-permute-start.14
  239.2 4.3 %collective-permute-start.15 = (bf16[48,768]{1,0:T(8,128)(2,1)S(1)}, bf16[48,768]{1,0:T(8,128)(2,1)S(1)}, u32[]{:S(2)}, u32[]{:S(2)}) collective-permute-start(bf16[48,768]{1,0:T(8,128)(2,1)S(1)} %fusion.24), channel_id=1, source_target_pairs={{0,4},{1,5},{2,6},{3,7},{4,8},{5,9},{6,10},{7,11},{16,20},{17,21},... | collective-permute-start | bytes 221192 | tf_op jit(solution)/shard_map/ppermute | solution.py:712
  244.1 2.0 collective-permute-done.15
  246.9 4.3 %collective-permute-start.20 = (bf16[8,192,768]{2,1,0:T(8,128)(2,1)}, bf16[8,192,768]{2,1,0:T(8,128)(2,1)S(1)}, u32[]{:S(2)}, u32[]{:S(2)}) collective-permute-start(bf16[8,192,768]{2,1,0:T(8,128)(2,1)} %copy-done.23), channel_id=1, source_target_pairs={{0,2},{1,3},{2,0},{3,1},{4,6},{5,7},{6,4},{7,5},{8,10},{9,11},{10,... | collective-permute-start | bytes 7077896 | tf_op jit(solution)/shard_map/ppermute | solution.py:768
  252.5 4.4 %collective-permute-start.16 = (bf16[48,768]{1,0:T(8,128)(2,1)S(1)}, bf16[48,768]{1,0:T(8,128)(2,1)S(1)}, u32[]{:S(2)}, u32[]{:S(2)}) collective-permute-start(bf16[48,768]{1,0:T(8,128)(2,1)S(1)} %get-tuple-element.156), channel_id=1, source_target_pairs={{0,4},{1,5},{2,6},{3,7},{4,8},{5,9},{6,10},{7,11},{8,12},{9,13},{1... | collective-permute-start | bytes 221192 | tf_op jit(solution)/shard_map/ppermute | solution.py:712
  256.9 3.1 select_convert_fusion.2
  260.5 4.2 %select_convert_fusion = bf16[8,48,3072]{2,1,0:T(8,128)(2,1)S(1)} fusion(bf16[8,48,3072]{2,1,0:T(8,128)(2,1)} %collective-permute-done.30, bf16[8,48,3072]{2,1,0:T(8,128)(2,1)S(1)} %copy-done.2, bf16[8,48,3072]{2,1,0:T(8,128)(2,1)} %collective-permute-done.29, bf16[8,48,3072]{2,1,0:T(8,128)(2,1)S(1)} %copy-done.6, pred[]{:T(512)S(6)} %eq.3), kind=kLoop, calls=%fused_computation | loop fusion | flops 9437184 | bytes 11796481 | tf_op jit(solution)/shard_map/convert_element_type | solution.py:797
  264.8 4.4 %collective-permute-start.31 = (bf16[2,48,3072]{2,1,0:T(8,128)(2,1)S(1)}, bf16[2,48,3072]{2,1,0:T(8,128)(2,1)S(1)}, u32[]{:S(2)}, u32[]{:S(2)}) collective-permute-start(bf16[2,48,3072]{2,1,0:T(8,128)(2,1)S(1)} %get-tuple-element.146), channel_id=1, source_target_pairs={{0,4},{1,5},{2,6},{3,7},{16,20},{17,21},{18,22},{19,23}} | collective-permute-start | bytes 1769480 | tf_op jit(solution)/shard_map/ppermute | solution.py:712
  270.0 8.2 %collective-permute-done.20 = bf16[8,192,768]{2,1,0:T(8,128)(2,1)S(1)} collective-permute-done((bf16[8,192,768]{2,1,0:T(8,128)(2,1)}, bf16[8,192,768]{2,1,0:T(8,128)(2,1)S(1)}, u32[]{:S(2)}, u32[]{:S(2)}) %collective-permute-start.20) | collective-permute-done | bytes 2359328 | tf_op jit(solution)/shard_map/ppermute | solution.py:768
  279.6 4.7 %collective-permute-start.22 = (bf16[2,192,768]{2,1,0:T(8,128)(2,1)S(1)}, bf16[2,192,768]{2,1,0:T(8,128)(2,1)S(1)}, u32[]{:S(2)}, u32[]{:S(2)}) collective-permute-start(bf16[2,192,768]{2,1,0:T(8,128)(2,1)S(1)} %get-tuple-element.150), channel_id=1, source_target_pairs={{0,4},{1,5},{2,6},{3,7},{16,20},{17,21},{18,22},{19,23}} | collective-permute-start | bytes 1769480 | tf_op jit(solution)/shard_map/ppermute | solution.py:712
  284.6 1.3 collective-permute-start.5
  286.8 9.1 %collective-permute-done.5 = bf16[144,768]{1,0:T(8,128)(2,1)S(1)} collective-permute-done((bf16[144,768]{1,0:T(8,128)(2,1)S(1)}, bf16[144,768]{1,0:T(8,128)(2,1)S(1)}, u32[]{:S(2)}, u32[]{:S(2)}) %collective-permute-start.5) | collective-permute-done | bytes 221216 | tf_op jit(solution)/shard_map/ppermute | solution.py:712
  295.9 4.4 %collective-permute-start.32 = (bf16[2,48,3072]{2,1,0:T(8,128)(2,1)S(1)}, bf16[2,48,3072]{2,1,0:T(8,128)(2,1)S(1)}, u32[]{:S(2)}, u32[]{:S(2)}) collective-permute-start(bf16[2,48,3072]{2,1,0:T(8,128)(2,1)S(1)} %fusion.3), channel_id=1, source_target_pairs={{0,4},{1,5},{2,6},{3,7},{4,8},{5,9},{6,10},{7,11},{16,20},{17,21},... | collective-permute-start | bytes 1769480 | tf_op jit(solution)/shard_map/ppermute | solution.py:712
  300.4 1.9 collective-permute-start.6
  303.1 15.6 %collective-permute-done.6 = bf16[144,768]{1,0:T(8,128)(2,1)S(1)} collective-permute-done((bf16[144,768]{1,0:T(8,128)(2,1)S(1)}, bf16[144,768]{1,0:T(8,128)(2,1)S(1)}, u32[]{:S(2)}, u32[]{:S(2)}) %collective-permute-start.6) | collective-permute-done | bytes 221216 | tf_op jit(solution)/shard_map/ppermute | solution.py:712
  319.6 4.4 %collective-permute-start.23 = (bf16[2,192,768]{2,1,0:T(8,128)(2,1)S(1)}, bf16[2,192,768]{2,1,0:T(8,128)(2,1)S(1)}, u32[]{:S(2)}, u32[]{:S(2)}) collective-permute-start(bf16[2,192,768]{2,1,0:T(8,128)(2,1)S(1)} %fusion.9), channel_id=1, source_target_pairs={{0,4},{1,5},{2,6},{3,7},{4,8},{5,9},{6,10},{7,11},{16,20},{17,21},... | collective-permute-start | bytes 1769480 | tf_op jit(solution)/shard_map/ppermute | solution.py:712
  327.3 9.0 %collective-permute-start.7 = (bf16[144,768]{1,0:T(8,128)(2,1)S(1)}, bf16[144,768]{1,0:T(8,128)(2,1)S(1)}, u32[]{:S(2)}, u32[]{:S(2)}) collective-permute-start(bf16[144,768]{1,0:T(8,128)(2,1)S(1)} %get-tuple-element.152), channel_id=1, source_target_pairs={{0,4},{1,5},{2,6},{3,7},{4,8},{5,9},{6,10},{7,11},{8,12},{9,13},{1... | collective-permute-start | bytes 663560 | tf_op jit(solution)/shard_map/ppermute | solution.py:712
  338.8 6.1 %collective-permute-start.33 = (bf16[2,48,3072]{2,1,0:T(8,128)(2,1)S(1)}, bf16[2,48,3072]{2,1,0:T(8,128)(2,1)S(1)}, u32[]{:S(2)}, u32[]{:S(2)}) collective-permute-start(bf16[2,48,3072]{2,1,0:T(8,128)(2,1)S(1)} %get-tuple-element.144), channel_id=1, source_target_pairs={{0,4},{1,5},{2,6},{3,7},{4,8},{5,9},{6,10},{7,11},{8,12},{9,13},{1... | collective-permute-start | bytes 1769480 | tf_op jit(solution)/shard_map/ppermute | solution.py:712
  345.0 1.3 collective-permute-start.36
  347.0 5.2 %collective-permute-start.24 = (bf16[2,192,768]{2,1,0:T(8,128)(2,1)S(1)}, bf16[2,192,768]{2,1,0:T(8,128)(2,1)S(1)}, u32[]{:S(2)}, u32[]{:S(2)}) collective-permute-start(bf16[2,192,768]{2,1,0:T(8,128)(2,1)S(1)} %get-tuple-element.148), channel_id=1, source_target_pairs={{0,4},{1,5},{2,6},{3,7},{4,8},{5,9},{6,10},{7,11},{8,12},{9,13},{1... | collective-permute-start | bytes 1769480 | tf_op jit(solution)/shard_map/ppermute | solution.py:712
  353.2 1.3 collective-permute-start.27
  354.5 2.9 collective-permute-done.36
  357.6 1.3 collective-permute-start.37
  359.5 5.5 %collective-permute-done.27 = bf16[2,192,768]{2,1,0:T(8,128)(2,1)S(1)} collective-permute-done((bf16[2,192,768]{2,1,0:T(8,128)(2,1)S(1)}, bf16[2,192,768]{2,1,0:T(8,128)(2,1)S(1)}, u32[]{:S(2)}, u32[]{:S(2)}) %collective-permute-start.27) | collective-permute-done | bytes 589856 | tf_op jit(solution)/shard_map/ppermute | solution.py:713
  366.2 5.8 %collective-permute-done.28 = bf16[192,768]{1,0:T(8,128)(2,1)S(1)} collective-permute-done((bf16[192,768]{1,0:T(8,128)(2,1)S(1)}, bf16[192,768]{1,0:T(8,128)(2,1)S(1)}, u32[]{:S(2)}, u32[]{:S(2)}) %collective-permute-start.28) | collective-permute-done | bytes 294944 | tf_op jit(solution)/shard_map/ppermute | solution.py:690
  (169 shorter events, 35.3 us)
Async XLA Ops:
  6.2 21.9 %copy-start.37 = (bf16[1,2,196,768]{3,1,2,0:T(2,128)(2,1)S(1)}, bf16[1,2,196,768]{3,1,2,0:T(2,128)(2,1)}, u32[]{:S(2)}) copy-start(bf16[1,2,196,768]{3,1,2,0:T(2,128)(2,1)} %param.13) | copy-start | bytes 1806340
  26.8 2.9 collective-permute-start
  29.7 22.1 %slice-start = ((s8[4718592]{0:T(1024)(128)(4,1)}), s8[4194304]{0:T(1024)(128)(4,1)S(1)}, s32[]{:S(2)}) async-start(s8[4718592]{0:T(1024)(128)(4,1)} %bitcast.129), calls=%async_computation | async-start | bytes 8388608
  30.6 14.8 %copy-start = (bf16[2,196,768]{2,1,0:T(8,128)(2,1)S(1)}, bf16[2,196,768]{2,1,0:T(8,128)(2,1)}, u32[]{:S(2)}) copy-start(bf16[2,196,768]{2,1,0:T(8,128)(2,1)} %copy.41.refs_3_) | copy-start | bytes 1806340
  30.6 21.1 %slice-start.1 = ((s8[4718592]{0:T(1024)(128)(4,1)}), s8[524288]{0:T(1024)(128)(4,1)S(1)}, s32[]{:S(2)}) async-start(s8[4718592]{0:T(1024)(128)(4,1)} %bitcast.129), calls=%async_computation.1 | async-start | bytes 1048576
  47.8 3.9 %copy-start.27 = (bf16[256,3072]{1,0:T(8,128)(2,1)S(1)}, bf16[256,3072]{1,0:T(8,128)(2,1)}, u32[]{:S(2)}) copy-start(bf16[256,3072]{1,0:T(8,128)(2,1)} %get-tuple-element.73.refs_2_) | copy-start | bytes 4718596
  51.8 3.4 copy-start.13
  58.6 51.1 %copy-start.26 = (bf16[288,3072]{1,0:T(8,128)(2,1)S(1)}, bf16[288,3072]{1,0:T(8,128)(2,1)}, u32[]{:S(2)}) copy-start(bf16[288,3072]{1,0:T(8,128)(2,1)} %get-tuple-element.86.refs_6_) | copy-start | bytes 5308420
  58.6 51.1 %copy-start.32 = (bf16[288,768]{1,0:T(8,128)(2,1)S(1)}, bf16[288,768]{1,0:T(8,128)(2,1)}, u32[]{:S(2)}) copy-start(bf16[288,768]{1,0:T(8,128)(2,1)} %get-tuple-element.85.refs_5_) | copy-start | bytes 1327108
  60.3 49.3 %collective-permute-start.1 = (bf16[2,196,768]{2,0,1:T(2,128)(2,1)S(1)}, bf16[2,196,768]{2,0,1:T(2,128)(2,1)S(1)}, u32[]{:S(2)}, u32[]{:S(2)}) collective-permute-start(bf16[2,196,768]{2,0,1:T(2,128)(2,1)S(1)} %copy.46), channel_id=1, source_target_pairs={{16,0},{17,1},{18,2},{19,3},{20,4},{21,5},{22,6},{23,7},{24,8},{25... | collective-permute-start | bytes 1806344 | tf_op jit(solution)/shard_map/ppermute | solution.py:783
  61.6 125.1 %collective-permute-start.12 = (bf16[8,48,768]{2,1,0:T(8,128)(2,1)}, bf16[8,48,768]{2,1,0:T(8,128)(2,1)}, u32[]{:S(2)}, u32[]{:S(2)}) collective-permute-start(bf16[8,48,768]{2,1,0:T(8,128)(2,1)} %get-tuple-element.113), channel_id=1, source_target_pairs={{16,17},{17,16},{18,19},{19,18},{20,21},{21,20},{22,23},{23,22},{2... | collective-permute-start | bytes 1769480 | tf_op jit(solution)/shard_map/ppermute | solution.py:768
  109.7 8.5 %copy-start.25 = (bf16[288,3072]{1,0:T(8,128)(2,1)S(1)}, bf16[288,3072]{1,0:T(8,128)(2,1)}, u32[]{:S(2)}) copy-start(bf16[288,3072]{1,0:T(8,128)(2,1)} %get-tuple-element.89.refs_2_) | copy-start | bytes 5308420
  109.7 8.5 %copy-start.31 = (bf16[288,768]{1,0:T(8,128)(2,1)S(1)}, bf16[288,768]{1,0:T(8,128)(2,1)}, u32[]{:S(2)}) copy-start(bf16[288,768]{1,0:T(8,128)(2,1)} %get-tuple-element.90.refs_3_) | copy-start | bytes 1327108
  115.7 1.5 copy-start.5
  118.2 14.7 %copy-start.16 = (f32[1,4,768]{2,1,0:T(4,128)S(1)}, f32[1,4,768]{2,1,0:T(4,128)}, u32[]{:S(2)}) copy-start(f32[1,4,768]{2,1,0:T(4,128)} %refs_2_.7) | copy-start | bytes 36868
  118.2 14.7 %copy-start.19 = (s32[2,196]{1,0:T(2,128)S(1)}, s32[2,196]{1,0:T(2,128)}, u32[]{:S(2)}) copy-start(s32[2,196]{1,0:T(2,128)} %refs_1_.11) | copy-start | bytes 4708
  150.6 39.7 %collective-permute-start.11 = (bf16[8,48,768]{2,1,0:T(8,128)(2,1)}, bf16[8,48,768]{2,1,0:T(8,128)(2,1)}, u32[]{:S(2)}, u32[]{:S(2)}) collective-permute-start(bf16[8,48,768]{2,1,0:T(8,128)(2,1)} %get-tuple-element.111), channel_id=1, source_target_pairs={{0,1},{1,0},{2,3},{3,2},{4,5},{5,4},{6,7},{7,6},{8,9},{9,8},{10,11... | collective-permute-start | bytes 1769480 | tf_op jit(solution)/shard_map/ppermute | solution.py:768
  155.4 1.5 copy-start.24
  161.2 85.7 %collective-permute-start.3 = (bf16[8,144,768]{2,1,0:T(8,128)(2,1)}, bf16[8,144,768]{2,1,0:T(8,128)(2,1)}, u32[]{:S(2)}, u32[]{:S(2)}) collective-permute-start(bf16[8,144,768]{2,1,0:T(8,128)(2,1)} %get-tuple-element.109), channel_id=1, source_target_pairs={{16,18},{17,19},{18,16},{19,17},{20,22},{21,23},{22,20},{23,21},{2... | collective-permute-start | bytes 5308424 | tf_op jit(solution)/shard_map/ppermute | solution.py:768
  163.1 7.9 %collective-permute-start.38 = (f32[16,768]{1,0:T(8,128)S(1)}, f32[16,768]{1,0:T(8,128)S(1)}, u32[]{:S(2)}, u32[]{:S(2)}) collective-permute-start(f32[16,768]{1,0:T(8,128)S(1)} %broadcast_select_fusion), channel_id=1, source_target_pairs={{0,1},{1,0},{2,3},{3,2},{4,5},{5,4},{6,7},{7,6},{8,9},{9,8},{10,11... | collective-permute-start | bytes 147464 | tf_op jit(solution)/shard_map/ppermute | solution.py:690
  170.9 4.3 %collective-permute-start.39 = (f32[16,768]{1,0:T(8,128)S(1)}, f32[16,768]{1,0:T(8,128)S(1)}, u32[]{:S(2)}, u32[]{:S(2)}) collective-permute-start(f32[16,768]{1,0:T(8,128)S(1)} %add.246), channel_id=1, source_target_pairs={{0,2},{1,3},{2,0},{3,1},{4,6},{5,7},{6,4},{7,5},{8,10},{9,11},{10,... | collective-permute-start | bytes 147464 | tf_op jit(solution)/shard_map/ppermute | solution.py:690
  173.0 87.1 %collective-permute-start.30 = (bf16[8,48,3072]{2,1,0:T(8,128)(2,1)}, bf16[8,48,3072]{2,1,0:T(8,128)(2,1)}, u32[]{:S(2)}, u32[]{:S(2)}) collective-permute-start(bf16[8,48,3072]{2,1,0:T(8,128)(2,1)} %copy-done.22), channel_id=1, source_target_pairs={{16,17},{17,16},{18,19},{19,18},{20,21},{21,20},{22,23},{23,22},{2... | collective-permute-start | bytes 7077896 | tf_op jit(solution)/shard_map/ppermute | solution.py:768
  175.3 7.9 %collective-permute-start.40 = (f32[16,768]{1,0:T(8,128)S(1)}, f32[16,768]{1,0:T(8,128)S(1)}, u32[]{:S(2)}, u32[]{:S(2)}) collective-permute-start(f32[16,768]{1,0:T(8,128)S(1)} %add.247), channel_id=1, source_target_pairs={{0,4},{1,5},{2,6},{3,7},{4,0},{5,1},{6,2},{7,3},{8,12},{9,13},{10,... | collective-permute-start | bytes 147464 | tf_op jit(solution)/shard_map/ppermute | solution.py:690
  179.0 13.9 %copy-start.38 = (bf16[8,48,768]{2,1,0:T(8,128)(2,1)S(1)}, bf16[8,48,768]{2,1,0:T(8,128)(2,1)}, u32[]{:S(2)}) copy-start(bf16[8,48,768]{2,1,0:T(8,128)(2,1)} %get-tuple-element.110) | copy-start | bytes 1769476
  183.2 11.3 %copy-start.9 = (bf16[8,144,768]{2,1,0:T(8,128)(2,1)}, bf16[8,144,768]{2,1,0:T(8,128)(2,1)S(1)}, u32[]{:S(2)}) copy-start(bf16[8,144,768]{2,1,0:T(8,128)(2,1)S(1)} %get-tuple-element.104) | copy-start | bytes 5308420
  183.2 77.3 %collective-permute-start.29 = (bf16[8,48,3072]{2,1,0:T(8,128)(2,1)}, bf16[8,48,3072]{2,1,0:T(8,128)(2,1)}, u32[]{:S(2)}, u32[]{:S(2)}) collective-permute-start(bf16[8,48,3072]{2,1,0:T(8,128)(2,1)} %get-tuple-element.119), channel_id=1, source_target_pairs={{0,1},{1,0},{2,3},{3,2},{4,5},{5,4},{6,7},{7,6},{8,9},{9,8},{10,11... | collective-permute-start | bytes 7077896 | tf_op jit(solution)/shard_map/ppermute | solution.py:768
  186.8 65.7 %collective-permute-start.2 = (bf16[8,144,768]{2,1,0:T(8,128)(2,1)}, bf16[8,144,768]{2,1,0:T(8,128)(2,1)}, u32[]{:S(2)}, u32[]{:S(2)}) collective-permute-start(bf16[8,144,768]{2,1,0:T(8,128)(2,1)} %get-tuple-element.105), channel_id=1, source_target_pairs={{0,2},{1,3},{2,0},{3,1},{4,6},{5,7},{6,4},{7,5},{8,10},{9,11},{10,... | collective-permute-start | bytes 5308424 | tf_op jit(solution)/shard_map/ppermute | solution.py:768
  190.2 5.3 %collective-permute-start.41 = (f32[16,768]{1,0:T(8,128)S(1)}, f32[16,768]{1,0:T(8,128)S(1)}, u32[]{:S(2)}, u32[]{:S(2)}) collective-permute-start(f32[16,768]{1,0:T(8,128)S(1)} %add.248), channel_id=1, source_target_pairs={{0,8},{1,9},{2,10},{3,11},{4,12},{5,13},{6,14},{7,15},{8,0},{9,1},... | collective-permute-start | bytes 147464 | tf_op jit(solution)/shard_map/ppermute | solution.py:690
  195.5 39.5 %collective-permute-start.13 = (bf16[4,48,768]{2,1,0:T(8,128)(2,1)S(1)}, bf16[4,48,768]{2,1,0:T(8,128)(2,1)S(1)}, u32[]{:S(2)}, u32[]{:S(2)}) collective-permute-start(bf16[4,48,768]{2,1,0:T(8,128)(2,1)S(1)} %dynamic-slice_bitcast_fusion.7), channel_id=1, source_target_pairs={{0,2},{1,3},{2,0},{3,1},{4,6},{5,7},{6,4},{7,5},{8,10},{9,11},{10,... | collective-permute-start | bytes 884744 | tf_op jit(solution)/shard_map/ppermute | solution.py:690
  196.0 39.0 %copy-start.36 = (bf16[8,48,768]{2,1,0:T(8,128)(2,1)S(1)}, bf16[8,48,768]{2,1,0:T(8,128)(2,1)}, u32[]{:S(2)}) copy-start(bf16[8,48,768]{2,1,0:T(8,128)(2,1)} %copy-done.35) | copy-start | bytes 1769476
  198.5 58.5 %copy-start.8 = (bf16[8,144,768]{2,1,0:T(8,128)(2,1)S(1)}, bf16[8,144,768]{2,1,0:T(8,128)(2,1)}, u32[]{:S(2)}) copy-start(bf16[8,144,768]{2,1,0:T(8,128)(2,1)} %copy-done.7) | copy-start | bytes 5308420
  198.5 58.5 %copy-start.10 = (bf16[8,144,768]{2,1,0:T(8,128)(2,1)S(1)}, bf16[8,144,768]{2,1,0:T(8,128)(2,1)}, u32[]{:S(2)}) copy-start(bf16[8,144,768]{2,1,0:T(8,128)(2,1)} %copy-done.9) | copy-start | bytes 5308420
  235.2 3.3 collective-permute-start.14
  238.5 0.7 collective-permute-start.17
  239.2 6.9 %collective-permute-start.15 = (bf16[48,768]{1,0:T(8,128)(2,1)S(1)}, bf16[48,768]{1,0:T(8,128)(2,1)S(1)}, u32[]{:S(2)}, u32[]{:S(2)}) collective-permute-start(bf16[48,768]{1,0:T(8,128)(2,1)S(1)} %fusion.24), channel_id=1, source_target_pairs={{0,4},{1,5},{2,6},{3,7},{4,8},{5,9},{6,10},{7,11},{16,20},{17,21},... | collective-permute-start | bytes 221192 | tf_op jit(solution)/shard_map/ppermute | solution.py:712
  246.1 23.2 %collective-permute-start.21 = (bf16[8,192,768]{2,1,0:T(8,128)(2,1)}, bf16[8,192,768]{2,1,0:T(8,128)(2,1)S(1)}, u32[]{:S(2)}, u32[]{:S(2)}) collective-permute-start(bf16[8,192,768]{2,1,0:T(8,128)(2,1)} %copy-done.21), channel_id=1, source_target_pairs={{16,18},{17,19},{18,16},{19,17},{20,22},{21,23},{22,20},{23,21},{2... | collective-permute-start | bytes 7077896 | tf_op jit(solution)/shard_map/ppermute | solution.py:768
  246.9 31.3 %collective-permute-start.20 = (bf16[8,192,768]{2,1,0:T(8,128)(2,1)}, bf16[8,192,768]{2,1,0:T(8,128)(2,1)S(1)}, u32[]{:S(2)}, u32[]{:S(2)}) collective-permute-start(bf16[8,192,768]{2,1,0:T(8,128)(2,1)} %copy-done.23), channel_id=1, source_target_pairs={{0,2},{1,3},{2,0},{3,1},{4,6},{5,7},{6,4},{7,5},{8,10},{9,11},{10,... | collective-permute-start | bytes 7077896 | tf_op jit(solution)/shard_map/ppermute | solution.py:768
  252.5 86.3 %collective-permute-start.16 = (bf16[48,768]{1,0:T(8,128)(2,1)S(1)}, bf16[48,768]{1,0:T(8,128)(2,1)S(1)}, u32[]{:S(2)}, u32[]{:S(2)}) collective-permute-start(bf16[48,768]{1,0:T(8,128)(2,1)S(1)} %get-tuple-element.156), channel_id=1, source_target_pairs={{0,4},{1,5},{2,6},{3,7},{4,8},{5,9},{6,10},{7,11},{8,12},{9,13},{1... | collective-permute-start | bytes 221192 | tf_op jit(solution)/shard_map/ppermute | solution.py:712
  256.9 3.6 copy-start.2
  256.9 3.6 copy-start.6
  260.1 24.2 %collective-permute-start.4 = (bf16[4,144,768]{2,1,0:T(8,128)(2,1)S(1)}, bf16[4,144,768]{2,1,0:T(8,128)(2,1)S(1)}, u32[]{:S(2)}, u32[]{:S(2)}) collective-permute-start(bf16[4,144,768]{2,1,0:T(8,128)(2,1)S(1)} %dynamic-slice_bitcast_fusion), channel_id=1, source_target_pairs={{0,1},{1,0},{2,3},{3,2},{4,5},{5,4},{6,7},{7,6},{8,9},{9,8},{10,11... | collective-permute-start | bytes 2654216 | tf_op jit(solution)/shard_map/ppermute | solution.py:690
  264.7 13.5 %copy-start.4 = (bf16[8,192,768]{2,1,0:T(8,128)(2,1)S(1)}, bf16[8,192,768]{2,1,0:T(8,128)(2,1)}, u32[]{:S(2)}) copy-start(bf16[8,192,768]{2,1,0:T(8,128)(2,1)} %copy-done.3) | copy-start | bytes 7077892
  264.8 21.1 %collective-permute-start.31 = (bf16[2,48,3072]{2,1,0:T(8,128)(2,1)S(1)}, bf16[2,48,3072]{2,1,0:T(8,128)(2,1)S(1)}, u32[]{:S(2)}, u32[]{:S(2)}) collective-permute-start(bf16[2,48,3072]{2,1,0:T(8,128)(2,1)S(1)} %get-tuple-element.146), channel_id=1, source_target_pairs={{0,4},{1,5},{2,6},{3,7},{16,20},{17,21},{18,22},{19,23}} | collective-permute-start | bytes 1769480 | tf_op jit(solution)/shard_map/ppermute | solution.py:712
  269.3 50.3 %collective-permute-start.34 = (bf16[2,48,3072]{2,1,0:T(8,128)(2,1)S(1)}, bf16[2,48,3072]{2,1,0:T(8,128)(2,1)S(1)}, u32[]{:S(2)}, u32[]{:S(2)}) collective-permute-start(bf16[2,48,3072]{2,1,0:T(8,128)(2,1)S(1)} %get-tuple-element.147), channel_id=1, source_target_pairs={{15,11},{14,10},{13,9},{12,8},{31,27},{30,26},{29,25},{28,24}} | collective-permute-start | bytes 1769480 | tf_op jit(solution)/shard_map/ppermute | solution.py:713
  279.6 20.8 %collective-permute-start.22 = (bf16[2,192,768]{2,1,0:T(8,128)(2,1)S(1)}, bf16[2,192,768]{2,1,0:T(8,128)(2,1)S(1)}, u32[]{:S(2)}, u32[]{:S(2)}) collective-permute-start(bf16[2,192,768]{2,1,0:T(8,128)(2,1)S(1)} %get-tuple-element.150), channel_id=1, source_target_pairs={{0,4},{1,5},{2,6},{3,7},{16,20},{17,21},{18,22},{19,23}} | collective-permute-start | bytes 1769480 | tf_op jit(solution)/shard_map/ppermute | solution.py:712
  284.6 11.3 %collective-permute-start.5 = (bf16[144,768]{1,0:T(8,128)(2,1)S(1)}, bf16[144,768]{1,0:T(8,128)(2,1)S(1)}, u32[]{:S(2)}, u32[]{:S(2)}) collective-permute-start(bf16[144,768]{1,0:T(8,128)(2,1)S(1)} %get-tuple-element.154), channel_id=1, source_target_pairs={{0,4},{1,5},{2,6},{3,7},{16,20},{17,21},{18,22},{19,23}} | collective-permute-start | bytes 663560 | tf_op jit(solution)/shard_map/ppermute | solution.py:712
  285.9 16.5 %collective-permute-start.8 = (bf16[144,768]{1,0:T(8,128)(2,1)S(1)}, bf16[144,768]{1,0:T(8,128)(2,1)S(1)}, u32[]{:S(2)}, u32[]{:S(2)}) collective-permute-start(bf16[144,768]{1,0:T(8,128)(2,1)S(1)} %get-tuple-element.155), channel_id=1, source_target_pairs={{15,11},{14,10},{13,9},{12,8},{31,27},{30,26},{29,25},{28,24}} | collective-permute-start | bytes 663560 | tf_op jit(solution)/shard_map/ppermute | solution.py:713
  295.9 28.2 %collective-permute-start.32 = (bf16[2,48,3072]{2,1,0:T(8,128)(2,1)S(1)}, bf16[2,48,3072]{2,1,0:T(8,128)(2,1)S(1)}, u32[]{:S(2)}, u32[]{:S(2)}) collective-permute-start(bf16[2,48,3072]{2,1,0:T(8,128)(2,1)S(1)} %fusion.3), channel_id=1, source_target_pairs={{0,4},{1,5},{2,6},{3,7},{4,8},{5,9},{6,10},{7,11},{16,20},{17,21},... | collective-permute-start | bytes 1769480 | tf_op jit(solution)/shard_map/ppermute | solution.py:712
  300.4 18.4 %collective-permute-start.6 = (bf16[144,768]{1,0:T(8,128)(2,1)S(1)}, bf16[144,768]{1,0:T(8,128)(2,1)S(1)}, u32[]{:S(2)}, u32[]{:S(2)}) collective-permute-start(bf16[144,768]{1,0:T(8,128)(2,1)S(1)} %fusion.18), channel_id=1, source_target_pairs={{0,4},{1,5},{2,6},{3,7},{4,8},{5,9},{6,10},{7,11},{16,20},{17,21},... | collective-permute-start | bytes 663560 | tf_op jit(solution)/shard_map/ppermute | solution.py:712
  302.5 22.6 %collective-permute-start.18 = (bf16[48,768]{1,0:T(8,128)(2,1)S(1)}, bf16[48,768]{1,0:T(8,128)(2,1)S(1)}, u32[]{:S(2)}, u32[]{:S(2)}) collective-permute-start(bf16[48,768]{1,0:T(8,128)(2,1)S(1)} %get-tuple-element.157), channel_id=1, source_target_pairs={{15,11},{14,10},{13,9},{12,8},{11,7},{10,6},{9,5},{8,4},{31,27},{3... | collective-permute-start | bytes 221192 | tf_op jit(solution)/shard_map/ppermute | solution.py:713
  318.8 8.5 %collective-permute-start.25 = (bf16[2,192,768]{2,1,0:T(8,128)(2,1)S(1)}, bf16[2,192,768]{2,1,0:T(8,128)(2,1)S(1)}, u32[]{:S(2)}, u32[]{:S(2)}) collective-permute-start(bf16[2,192,768]{2,1,0:T(8,128)(2,1)S(1)} %get-tuple-element.151), channel_id=1, source_target_pairs={{15,11},{14,10},{13,9},{12,8},{31,27},{30,26},{29,25},{28,24}} | collective-permute-start | bytes 1769480 | tf_op jit(solution)/shard_map/ppermute | solution.py:713
  319.6 16.7 %collective-permute-start.23 = (bf16[2,192,768]{2,1,0:T(8,128)(2,1)S(1)}, bf16[2,192,768]{2,1,0:T(8,128)(2,1)S(1)}, u32[]{:S(2)}, u32[]{:S(2)}) collective-permute-start(bf16[2,192,768]{2,1,0:T(8,128)(2,1)S(1)} %fusion.9), channel_id=1, source_target_pairs={{0,4},{1,5},{2,6},{3,7},{4,8},{5,9},{6,10},{7,11},{16,20},{17,21},... | collective-permute-start | bytes 1769480 | tf_op jit(solution)/shard_map/ppermute | solution.py:712
  324.1 1.8 collective-permute-start.9
  325.1 12.8 %collective-permute-start.35 = (bf16[2,48,3072]{2,1,0:T(8,128)(2,1)S(1)}, bf16[2,48,3072]{2,1,0:T(8,128)(2,1)S(1)}, u32[]{:S(2)}, u32[]{:S(2)}) collective-permute-start(bf16[2,48,3072]{2,1,0:T(8,128)(2,1)S(1)} %get-tuple-element.145), channel_id=1, source_target_pairs={{15,11},{14,10},{13,9},{12,8},{11,7},{10,6},{9,5},{8,4},{31,27},{3... | collective-permute-start | bytes 1769480 | tf_op jit(solution)/shard_map/ppermute | solution.py:713
  325.9 19.1 %collective-permute-start.19 = (bf16[48,768]{1,0:T(8,128)(2,1)S(1)}, bf16[48,768]{1,0:T(8,128)(2,1)S(1)}, u32[]{:S(2)}, u32[]{:S(2)}) collective-permute-start(bf16[48,768]{1,0:T(8,128)(2,1)S(1)} %fusion.23), channel_id=1, source_target_pairs={{15,11},{14,10},{13,9},{12,8},{11,7},{10,6},{9,5},{8,4},{7,3},{6,2... | collective-permute-start | bytes 221192 | tf_op jit(solution)/shard_map/ppermute | solution.py:713
  327.3 19.7 %collective-permute-start.7 = (bf16[144,768]{1,0:T(8,128)(2,1)S(1)}, bf16[144,768]{1,0:T(8,128)(2,1)S(1)}, u32[]{:S(2)}, u32[]{:S(2)}) collective-permute-start(bf16[144,768]{1,0:T(8,128)(2,1)S(1)} %get-tuple-element.152), channel_id=1, source_target_pairs={{0,4},{1,5},{2,6},{3,7},{4,8},{5,9},{6,10},{7,11},{8,12},{9,13},{1... | collective-permute-start | bytes 663560 | tf_op jit(solution)/shard_map/ppermute | solution.py:712
  336.3 15.8 %collective-permute-start.10 = (bf16[144,768]{1,0:T(8,128)(2,1)S(1)}, bf16[144,768]{1,0:T(8,128)(2,1)S(1)}, u32[]{:S(2)}, u32[]{:S(2)}) collective-permute-start(bf16[144,768]{1,0:T(8,128)(2,1)S(1)} %fusion.17), channel_id=1, source_target_pairs={{15,11},{14,10},{13,9},{12,8},{11,7},{10,6},{9,5},{8,4},{7,3},{6,2... | collective-permute-start | bytes 663560 | tf_op jit(solution)/shard_map/ppermute | solution.py:713
  338.0 15.0 %collective-permute-start.26 = (bf16[2,192,768]{2,1,0:T(8,128)(2,1)S(1)}, bf16[2,192,768]{2,1,0:T(8,128)(2,1)S(1)}, u32[]{:S(2)}, u32[]{:S(2)}) collective-permute-start(bf16[2,192,768]{2,1,0:T(8,128)(2,1)S(1)} %get-tuple-element.149), channel_id=1, source_target_pairs={{15,11},{14,10},{13,9},{12,8},{11,7},{10,6},{9,5},{8,4},{31,27},{3... | collective-permute-start | bytes 1769480 | tf_op jit(solution)/shard_map/ppermute | solution.py:713
  338.8 15.6 %collective-permute-start.33 = (bf16[2,48,3072]{2,1,0:T(8,128)(2,1)S(1)}, bf16[2,48,3072]{2,1,0:T(8,128)(2,1)S(1)}, u32[]{:S(2)}, u32[]{:S(2)}) collective-permute-start(bf16[2,48,3072]{2,1,0:T(8,128)(2,1)S(1)} %get-tuple-element.144), channel_id=1, source_target_pairs={{0,4},{1,5},{2,6},{3,7},{4,8},{5,9},{6,10},{7,11},{8,12},{9,13},{1... | collective-permute-start | bytes 1769480 | tf_op jit(solution)/shard_map/ppermute | solution.py:712
  345.0 12.4 %collective-permute-start.36 = (bf16[2,48,3072]{2,1,0:T(8,128)(2,1)S(1)}, bf16[2,48,3072]{2,1,0:T(8,128)(2,1)S(1)}, u32[]{:S(2)}, u32[]{:S(2)}) collective-permute-start(bf16[2,48,3072]{2,1,0:T(8,128)(2,1)S(1)} %fusion.2), channel_id=1, source_target_pairs={{15,11},{14,10},{13,9},{12,8},{11,7},{10,6},{9,5},{8,4},{7,3},{6,2... | collective-permute-start | bytes 1769480 | tf_op jit(solution)/shard_map/ppermute | solution.py:713
  347.0 12.5 %collective-permute-start.24 = (bf16[2,192,768]{2,1,0:T(8,128)(2,1)S(1)}, bf16[2,192,768]{2,1,0:T(8,128)(2,1)S(1)}, u32[]{:S(2)}, u32[]{:S(2)}) collective-permute-start(bf16[2,192,768]{2,1,0:T(8,128)(2,1)S(1)} %get-tuple-element.148), channel_id=1, source_target_pairs={{0,4},{1,5},{2,6},{3,7},{4,8},{5,9},{6,10},{7,11},{8,12},{9,13},{1... | collective-permute-start | bytes 1769480 | tf_op jit(solution)/shard_map/ppermute | solution.py:712
  353.2 11.8 %collective-permute-start.27 = (bf16[2,192,768]{2,1,0:T(8,128)(2,1)S(1)}, bf16[2,192,768]{2,1,0:T(8,128)(2,1)S(1)}, u32[]{:S(2)}, u32[]{:S(2)}) collective-permute-start(bf16[2,192,768]{2,1,0:T(8,128)(2,1)S(1)} %fusion.8), channel_id=1, source_target_pairs={{15,11},{14,10},{13,9},{12,8},{11,7},{10,6},{9,5},{8,4},{7,3},{6,2... | collective-permute-start | bytes 1769480 | tf_op jit(solution)/shard_map/ppermute | solution.py:713
  357.6 7.7 %collective-permute-start.37 = (bf16[48,3072]{1,0:T(8,128)(2,1)S(1)}, bf16[48,3072]{1,0:T(8,128)(2,1)S(1)}, u32[]{:S(2)}, u32[]{:S(2)}) collective-permute-start(bf16[48,3072]{1,0:T(8,128)(2,1)S(1)} %dynamic-slice_bitcast_fusion.5), channel_id=1, source_target_pairs={{0,2},{1,3},{2,0},{3,1},{4,6},{5,7},{6,4},{7,5},{8,10},{9,11},{10,... | collective-permute-start | bytes 884744 | tf_op jit(solution)/shard_map/ppermute | solution.py:690
  365.2 6.8 %collective-permute-start.28 = (bf16[192,768]{1,0:T(8,128)(2,1)S(1)}, bf16[192,768]{1,0:T(8,128)(2,1)S(1)}, u32[]{:S(2)}, u32[]{:S(2)}) collective-permute-start(bf16[192,768]{1,0:T(8,128)(2,1)S(1)} %dynamic-slice_bitcast_fusion.6), channel_id=1, source_target_pairs={{0,1},{1,0},{2,3},{3,2},{4,5},{5,4},{6,7},{7,6},{8,9},{9,8},{10,11... | collective-permute-start | bytes 884744 | tf_op jit(solution)/shard_map/ppermute | solution.py:690
  (19 other events, 20.7 us)
